TPU v7x, 768 devices: a whole 4x8x12 slice. The times are simulated.
768 devices in a mesh: group: 24 (over z, core), route: 32 (over x, y).
Axes of the slice: x: 4, y: 8, z: 12, core: 2. Of those that a mesh axis runs over, the one named last changes fastest.
Arguments:
- ensemble: bfloat16 [256, 98304], P('route', 'group')
- obs_anom: bfloat16 [256, 98304], P(None, ('group', 'route')), may hold values from -6 to 6
- obs_weight: bfloat16 [256, 98304], P(None, ('group', 'route')), may hold values from -1.5 to 1.5
- taper_table: float32 [16, 128, 128], replicated, may hold values from 0.05 to 1
- pair_obs: int32 [24, 32, 32], P('group', 'route'), may hold values from 0 to 23
- pair_tile: int32 [24, 32, 32], P('group', 'route'), may hold values from 0 to 31
- pair_taper: int32 [24, 32, 32], P('group', 'route'), may hold values from 0 to 15
- pair_count: int32 [24, 32], P('group', 'route'), may hold values from 1 to 32, as said below
Outputs:
- updated: bfloat16 [256, 98304], P('route', 'group')
Inputs may be any that keep to these rules, and one draw needn't show every extreme that they name: The first pair_count[g, r] pairs of list (g, r) are live; in every draw some list has exactly 32 live pairs.
All inputs are finite; a program needn't handle non-finite values.
Results may differ from a plain program's by a relative error of at most 0.0075.
Values may be sent and summed in bfloat16 or wider, within the bound.
No kernel may reach another device: no remote copies, remote signals or barrier semaphores. Data moves between devices by JAX's collectives and lax.ppermute only.
A program may use at most 32 MiB of HBM per device.

v0:
```python
import jax
import jax.numpy as jnp
from jax import lax
from jax.sharding import PartitionSpec as P


def on_device(
    ensemble, obs_anom, obs_weight, taper_table, pair_obs, pair_tile, pair_taper, pair_count
):
    routes = lax.axis_size("route")
    groups = lax.axis_size("group")
    local_members = ensemble.shape[0]
    members = local_members * routes
    tile_width = ensemble.shape[1] // routes
    block_width = obs_anom.shape[1]
    row_sums = jnp.sum(ensemble.astype(jnp.float32), axis=0)
    member_total = lax.psum(row_sums, "route")
    centre_row = member_total / members
    anomaly = (ensemble.astype(jnp.float32) - centre_row[None, :]).astype(jnp.bfloat16)
    anomaly_panel = lax.all_gather(anomaly, "route", axis=0, tiled=True)
    column_y, column_w = (
        lax.all_gather(obs_anom, "group", axis=1, tiled=True),
        lax.all_gather(obs_weight, "group", axis=1, tiled=True),
    )
    column_y = column_y.reshape(members, groups, block_width)
    column_w = column_w.reshape(members, groups, block_width)
    tiled_panel = anomaly_panel.reshape(members, routes, tile_width)
    pair_blocks = pair_obs[0, 0]
    pair_tiles = pair_tile[0, 0]
    pair_kinds = pair_taper[0, 0]
    live_count = pair_count[0, 0]
    a_pairs = jnp.take(tiled_panel, pair_tiles, axis=1)
    y_pairs = jnp.take(column_y, pair_blocks, axis=1)
    w_pairs = jnp.take(column_w, pair_blocks, axis=1)
    cross = jnp.einsum("mqi,mqj->qij", a_pairs, y_pairs, preferred_element_type=jnp.float32)
    is_live = jnp.arange(pair_blocks.shape[0]) < live_count
    tapers = jnp.take(taper_table, pair_kinds, axis=0)
    gain_blocks = jnp.where(is_live[:, None, None], tapers * cross / (members - 1), 0.0).astype(
        jnp.bfloat16
    )
    weighted = jnp.einsum("mqj,qij->qmi", w_pairs, gain_blocks, preferred_element_type=jnp.float32)
    summed = jax.ops.segment_sum(weighted, pair_tiles, num_segments=routes)
    update = lax.psum_scatter(
        jnp.transpose(summed, (1, 0, 2))
        .reshape(local_members * lax.axis_size("route"), routes * tile_width)
        .astype(jnp.bfloat16),
        "route",
        scatter_dimension=0,
        tiled=True,
    ).astype(jnp.float32)
    return (ensemble.astype(jnp.float32) + update).astype(jnp.bfloat16)


def solution(mesh):
    placed = (
        P("route", "group"),
        P(None, ("group", "route")),
        P(None, ("group", "route")),
        P(),
        P("group", "route", None),
        P("group", "route", None),
        P("group", "route", None),
        P("group", "route"),
    )
    return jax.shard_map(
        on_device, mesh=mesh, in_specs=placed, out_specs=P("route", "group"), check_vma=False
    )
```

profile of v0, /device:TPU:1, one launch (start us, length us, event | category | flops | bytes accessed | tf_op | source)
XLA Modules:
  0.0 510.6 jit_solution(3116352362652703392)
XLA Ops:
  6.5 0.0 copy-start
  6.5 0.0 all-gather.8.cloned.1.call-start
  6.5 1.6 copy.22
  8.2 0.0 all-gather.8.cloned.1.call-update
  8.2 0.0 all-gather.4.cloned.1.call-start
  8.3 1.6 copy.18
  9.8 0.0 all-gather.4.cloned.1.call-update
  9.9 0.0 all-gather.6.cloned.1.call-start
  9.9 0.9 convert_reduce_fusion
  10.8 116.5 %psum.7 = f32[4096]{0:T(1024)S(1)} all-reduce(f32[4096]{0:T(1024)S(1)} %convert_reduce_fusion), channel_id=1, replica_groups=mesh['group'=24,'route'=32] {'route'}, use_global_device_ids=true, to_apply=%region_1.3 | all-reduce | flops 4096 | bytes 32768 | tf_op jit(solution)/shard_map/psum | solution.py:17
  127.3 1.5 fusion.26
  128.7 0.0 all-gather.6.cloned.1.call-update
  128.8 0.0 reduce-scatter.4.cloned.1.call-start
  129.5 0.7 fusion.28
  130.1 0.0 copy-done
  130.1 0.0 copy-start.4
  130.1 0.0 copy-start.2
  130.2 0.0 copy-start.3
  130.2 2.0 gather_fusion
  132.2 0.0 copy-done.4
  132.2 0.0 copy-done.2
  132.2 0.0 copy-done.3
  132.3 0.0 all-gather.8.cloned.1.call-done
  132.3 1.9 copy.23
  134.2 2.5 all-gather.4.cloned.1.call-done
  136.7 2.6 copy.19
  139.3 3.6 gather_fusion.2
  142.9 2.2 gather_fusion.3
  145.1 95.6 %all-gather.6.cloned.1.call-done = bf16[256,4096]{1,0:T(8,128)(2,1)} async-done(((bf16[8,4096]{1,0:T(8,128)(2,1)}), bf16[256,4096]{1,0:T(8,128)(2,1)}) %all-gather.6.cloned.1.call-update) | async-done | bytes 2097168 | tf_op jit(solution)/shard_map/all_gather | solution.py:20
  240.7 4.1 copy.20
  244.7 3.2 copy.21
  247.9 2.1 gather_fusion.1
  250.1 7.0 %fusion.3 = f32[32,256,128]{2,1,0:T(8,128)} fusion(bf16[32,256,128]{2,1,0:T(8,128)(2,1)} %gather_fusion.2, pred[32]{0:T(512)(128)(4,1)S(1)} %get-tuple-element.6, f32[32,128,128]{2,1,0:T(8,128)} %gather_fusion, bf16[32,256,128]{2,1,0:T(8,128)(2,1)} %gather_fusion.3, bf16[32,256,128]{2,1,0:T(8,128)(2,1)} %gather_fusion.1, ...), kind=kOutput, calls=%fused_computation.8 | convolution fusion | flops 542638080 | bytes 12583040 | tf_op jit(solution)/shard_map/mqj,qij->qmi/dot_general | solution.py:41
  257.1 2.5 broadcast_in_dim.46
  259.5 9.9 %scatter_fusion = f32[32,256,128]{2,1,0:T(8,128)} fusion(f32[32,256,128]{2,1,0:T(8,128)} %broadcast_in_dim.46, s32[32]{0:T(128)S(1)} %bitcast.46, f32[32,256,128]{2,1,0:T(8,128)} %fusion.3), kind=kCustom, calls=%fused_computation.4 | custom fusion | flops 1048576 | bytes 12583040 | tf_op jit(solution)/shard_map/scatter-add | solution.py:42
  269.4 2.5 convert_bitcast_fusion
  271.9 2.9 copy.25
  274.8 4.1 copy.28
  278.9 0.0 copy-start.1
  278.9 0.0 reduce-scatter.4.cloned.1.call-update
  279.0 223.6 %reduce-scatter.4.cloned.1.call-done = bf16[8,4096]{1,0:T(8,128)(2,1)} async-done(((bf16[256,4096]{1,0:T(8,128)(2,1)}), bf16[8,4096]{1,0:T(8,128)(2,1)}) %reduce-scatter.4.cloned.1.call-update) | async-done | bytes 65552 | tf_op jit(solution)/shard_map/reduce_scatter | solution.py:43
  502.5 0.0 copy-done.1
  502.5 1.5 fusion.27
  (8 shorter events, 0.1 us)
Async XLA Ops:
  6.5 123.6 %copy-start = (f32[16,128,128]{2,1,0:T(8,128)S(1)}, f32[16,128,128]{2,1,0:T(8,128)}, u32[]{:S(2)}) copy-start(f32[16,128,128]{2,1,0:T(8,128)} %param.13) | copy-start | bytes 3145732
  6.5 125.8 %all-gather.8.cloned.1.call-start = ((), (), s32[]{:S(2)}) async-start(), calls=%async_computation.3 | async-start | bytes 1638400 | tf_op jit(solution)/shard_map/all_gather | solution.py:22
  8.2 128.5 %all-gather.4.cloned.1.call-start = ((), (), s32[]{:S(2)}) async-start(), calls=%async_computation.1 | async-start | bytes 1638400 | tf_op jit(solution)/shard_map/all_gather | solution.py:23
  9.9 230.8 %all-gather.6.cloned.1.call-start = ((), (), s32[]{:S(2)}) async-start(), calls=%async_computation.2 | async-start | bytes 2162688 | tf_op jit(solution)/shard_map/all_gather | solution.py:20
  128.8 373.8 %reduce-scatter.4.cloned.1.call-start = ((), (), s32[]{:S(2)}) async-start(), calls=%async_computation.4 | async-start | bytes 2162688 | tf_op jit(solution)/shard_map/reduce_scatter | solution.py:43
  130.1 2.0 copy-start.4
  130.1 2.1 copy-start.2
  130.2 2.1 copy-start.3
  278.9 223.6 %copy-start.1 = (bf16[8,4096]{1,0:T(8,128)(2,1)S(1)}, bf16[8,4096]{1,0:T(8,128)(2,1)}, u32[]{:S(2)}) copy-start(bf16[8,4096]{1,0:T(8,128)(2,1)} %param.10) | copy-start | bytes 196612
Sparse Core Ops, SparseCore 0:
  9.8 67.7 all-gather.7
  80.1 56.6 all-gather.3
  140.5 100.1 all-gather.5
  279.1 223.3 reduce-scatter.3
where the time goes:
time: 515 us; the launch traced here: 511 us
  waiting for transfers between devices  322 us (63%)
  blocking collectives  116 us (23%)
  local copies, waits for them, and re-layouts  34.5 us (7%)
  other arithmetic  16.9 us (3%)
  between operations  13.9 us (3%)
  matrix products  6.98 us (1%)
    reduce_scatter x1, waiting for transfers between devices, on_device(): lax.psum_scatter(jnp.transpose(summed, (1, 0, 2)).reshape(local_members *...  224 us
    psum x1, blocking collectives, on_device(): member_total = lax.psum(row_sums, 'route')  116 us
    all_gather x1, waiting for transfers between devices, on_device(): anomaly_panel = lax.all_gather(anomaly, 'route', axis=0, tiled=True)  95.6 us
  transfers between devices with their start and end apart: 4, of which 3 were waited for; matrix products, arithmetic and copies ran while one was open for 3% of the time, Pallas kernels for 0%

commit v1 on v0

v1 whole, which is shorter than its diff:
```python
import jax
import jax.numpy as jnp
from jax import lax
from jax.experimental import pallas as pl
from jax.experimental.pallas import tpu as pltpu
from jax.sharding import Mesh, PartitionSpec as P

Z, CORE, X, Y = 12, 2, 4, 8
UNROLL = 4


def pair_kernel(
    tile_ref, obs_ref, kind_ref, count_ref, core_ref,
    panel_ref, own_ref, other_ref, taper_ref, out_ref, anom_ref, acc_ref,
):
    tiles, members, width = acc_ref.shape

    @pl.loop(0, tiles)
    def _(t):
        cells = panel_ref[:, pl.ds(pl.multiple_of(t * width, width), width)].astype(jnp.float32)
        centre = jnp.sum(cells, axis=0, keepdims=True) * (1.0 / members)
        anom_ref[t] = (cells - centre).astype(jnp.bfloat16)
        acc_ref[t] = jnp.zeros((members, width), jnp.float32)

    count = count_ref[0]
    core = core_ref[0]

    @pl.loop(0, lax.div(count + (UNROLL - 1), UNROLL))
    def _(step):
        terms = []
        for u in range(UNROLL):
            q = step * UNROLL + u
            t, j, k = tile_ref[q], obs_ref[q], kind_ref[q]
            z = lax.shift_right_logical(j, 1)
            mine = (j & 1) == core
            y_low = jnp.where(mine, own_ref[z, 0:128], other_ref[z, 0:128])
            y_high = jnp.where(mine, own_ref[z, 128:256], other_ref[z, 128:256])
            w = jnp.where(mine, own_ref[z, 256:512], other_ref[z, 256:512])
            y = jnp.concatenate([y_low, y_high], axis=1)
            cross = jnp.dot(y, anom_ref[t], preferred_element_type=jnp.float32)
            gain = jnp.where(q < count, taper_ref[k] * cross, 0.0).astype(jnp.bfloat16)
            terms.append((t, jnp.dot(w, gain, preferred_element_type=jnp.float32)))
        for t, term in terms:
            acc_ref[t] += term

    @pl.loop(0, tiles)
    def _(t):
        out_ref[:, pl.ds(pl.multiple_of(t * width, width), width)] = acc_ref[t].astype(jnp.bfloat16)


def on_device(
    ensemble, obs_anom, obs_weight, taper_table, pair_obs, pair_tile, pair_taper, pair_count
):
    rows, cells = ensemble.shape
    members = rows * X * Y
    width = obs_anom.shape[1]
    half = members // 2
    blocks = jnp.concatenate([obs_anom[:half].T, obs_anom[half:].T, obs_weight], axis=0)
    own = lax.all_gather(blocks, "z", axis=0)
    other = lax.ppermute(own, "core", [(0, 1), (1, 0)])
    part = lax.all_to_all(jnp.broadcast_to(ensemble[None], (Y, rows, cells)), "y", 0, 0, tiled=True)
    part = part.reshape(1, Y * rows, cells)
    panel = lax.all_to_all(jnp.broadcast_to(part, (X, Y * rows, cells)), "x", 0, 0, tiled=True)
    panel = panel.reshape(members, cells)
    tapers = jnp.swapaxes(taper_table, 1, 2) * (1.0 / (members - 1))
    smem = pl.BlockSpec(memory_space=pltpu.SMEM)
    vmem = pl.BlockSpec(memory_space=pltpu.VMEM)
    partial = pl.pallas_call(
        pair_kernel,
        out_shape=jax.ShapeDtypeStruct((members, cells), jnp.bfloat16),
        in_specs=[smem] * 5 + [vmem] * 4,
        out_specs=vmem,
        scratch_shapes=[
            pltpu.VMEM((cells // width, members, width), jnp.bfloat16),
            pltpu.VMEM((cells // width, members, width), jnp.float32),
        ],
        compiler_params=pltpu.CompilerParams(vmem_limit_bytes=40 * 2**20),
        name="pairs",
    )(
        pair_tile[0, 0], pair_obs[0, 0], pair_taper[0, 0], pair_count[0],
        lax.axis_index("core").reshape(1), panel, own, other, tapers,
    )
    sent = lax.all_to_all(partial.reshape(X, Y * rows, cells), "x", 0, 0, tiled=True)
    summed = jnp.sum(sent.astype(jnp.float32), axis=0).astype(jnp.bfloat16)
    sent = lax.all_to_all(summed.reshape(Y, rows, cells), "y", 0, 0, tiled=True)
    update = jnp.sum(sent.astype(jnp.float32), axis=0)
    return (ensemble.astype(jnp.float32) + update).astype(jnp.bfloat16)


def solution(mesh):
    fine = Mesh(mesh.devices.reshape(Z, CORE, X, Y), ("z", "core", "x", "y"))
    group, route = ("z", "core"), ("x", "y")
    placed = (
        P(route, group),
        P(None, group + route),
        P(None, group + route),
        P(),
        P(group, route, None),
        P(group, route, None),
        P(group, route, None),
        P(group, route),
    )
    return jax.shard_map(
        on_device, mesh=fine, in_specs=placed, out_specs=P(route, group), check_vma=False
    )
```

time: 515 us -> 153 us (0.30)
  waiting for transfers between devices: 322 us -> 32.3 us
  blocking collectives: 116 us -> 72 us
  local copies, waits for them, and re-layouts: 34.5 us -> 6.27 us
  starting transfers between devices: 0.13 us -> 16.8 us
  other arithmetic: 16.9 us -> 3.91 us
  matrix products: 6.98 us -> 0 us
  Pallas kernels: 0 us -> 6.18 us
    reduce_scatter x1 -> x0, waiting for transfers between devices: 224 us -> none  [on_device(): lax.psum_scatter(jnp.transpose(summed, (1, 0, 2)).reshape(local_members *...]
    psum x1 -> x0, blocking collectives: 116 us -> none  [on_device(): member_total = lax.psum(row_sums, 'route')]
    all_to_all x0 -> x3, blocking collectives: none -> 72 us  [the longest x1 27.9 us: on_device(): lax.all_to_all(partial.reshape(X, Y * rows, cells), 'x', 0, 0, tiled=True)]
    all_gather x3 -> x1, waiting for transfers between devices: 98.1 us -> 32.3 us  [on_device(): own = lax.all_gather(blocks, 'z', axis=0)]
    gather x4 -> x0, local copies, waits for them, and re-layouts: 9.9 us -> none  [the longest x1 3.58 us: on_device(): w_pairs = jnp.take(column_w, pair_blocks, axis=1)]
    scatter-add x1 -> x0, other arithmetic: 9.87 us -> none  [on_device(): summed = jax.ops.segment_sum(weighted, pair_tiles, num_segments=routes)]
    ppermute x0 -> x1, starting transfers between devices: none -> 8.92 us  [on_device(): other = lax.ppermute(own, 'core', [(0, 1), (1, 0)])]
    all_to_all x0 -> x1, starting transfers between devices: none -> 7.93 us  [on_device(): lax.all_to_all(jnp.broadcast_to(part, (X, Y * rows, cells)), 'x', 0, 0, t...]
  transfers between devices with their start and end apart: 4 -> 3, of which waited for: 3 -> 1; matrix products, arithmetic and copies ran while one was open for 3% -> 3% of each run, Pallas kernels for 0% -> 0%
where the time goes in v1:
time: 153 us; the launch traced here: 152 us
  blocking collectives  72 us (47%)
  waiting for transfers between devices  32.3 us (21%)
  starting transfers between devices  16.8 us (11%)
  between operations  14.2 us (9%)
  local copies, waits for them, and re-layouts  6.27 us (4%)
  Pallas kernels  6.18 us (4%)
  other arithmetic  3.91 us (3%)
    all_gather x1, waiting for transfers between devices, on_device(): own = lax.all_gather(blocks, 'z', axis=0)  32.3 us
    all_to_all x1, blocking collectives, on_device(): lax.all_to_all(partial.reshape(X, Y * rows, cells), 'x', 0, 0, tiled=True)  27.9 us
    all_to_all x1, blocking collectives, on_device(): sent = lax.all_to_all(summed.reshape(Y, rows, cells), 'y', 0, 0, tiled=True)  24.5 us
    all_to_all x1, blocking collectives, on_device(): lax.all_to_all(jnp.broadcast_to(ensemble[None], (Y, rows, cells)), 'y', 0...  19.7 us
    ppermute x1, starting transfers between devices, on_device(): other = lax.ppermute(own, 'core', [(0, 1), (1, 0)])  8.92 us
    all_to_all x1, starting transfers between devices, on_device(): lax.all_to_all(jnp.broadcast_to(part, (X, Y * rows, cells)), 'x', 0, 0, t...  7.93 us
    pallas_call x1, Pallas kernels, on_device(): pl.pallas_call(pair_kernel, out_shape=jax.ShapeDtypeStruct((members, cell...  6.18 us
  transfers between devices with their start and end apart: 3, of which 1 were waited for; matrix products, arithmetic and copies ran while one was open for 3% of the time, Pallas kernels for 0%

profile of v1, /device:TPU:1, one launch (start us, length us, event | category | flops | bytes accessed | tf_op | source)
XLA Modules:
  0.0 151.7 jit_solution(2697326459261157491)
XLA Ops:
  6.5 0.0 all-gather.3.cloned.1.call-start
  6.5 0.8 fusion
  7.3 0.1 copy.15
  7.4 0.1 copy.16
  7.6 1.5 pad_maximum_fusion
  9.1 0.0 all-gather.3.cloned.1.call-update
  9.1 0.9 broadcast_in_dim.6
  10.0 19.7 %all_to_all.20 = bf16[8,8,4096]{2,1,0:T(8,128)(2,1)S(1)} all-to-all(bf16[8,8,4096]{2,1,0:T(8,128)(2,1)S(1)} %broadcast_in_dim.6), channel_id=1, replica_groups=mesh['z'=12,'core'=2,'x'=4,'y'=8] {'y'}, dimensions={0} | all-to-all | bytes 1048576 | tf_op jit(solution)/shard_map/all_to_all | solution.py:61
  29.6 1.6 %broadcast_in_dim.15 = bf16[4,64,4096]{2,1,0:T(8,128)(2,1)} broadcast(bf16[64,4096]{1,0:T(8,128)(2,1)S(1)} %bitcast.22), dimensions={1,2} | broadcast | bytes 2621440 | tf_op jit(solution)/shard_map/broadcast_in_dim | solution.py:63
  31.2 0.0 copy-start.4
  31.2 7.9 %all-to-all-start.1 = ((bf16[4,64,4096]{2,1,0:T(8,128)(2,1)}), bf16[4,64,4096]{2,1,0:T(8,128)(2,1)S(1)}, u32[]{:S(2)}, u32[]{:S(2)}) async-start(bf16[4,64,4096]{2,1,0:T(8,128)(2,1)} %broadcast_in_dim.15), calls=%async_computation.1 | async-start | bytes 4194304 | tf_op jit(solution)/shard_map/all_to_all | solution.py:63
  39.2 32.3 %all-gather.3.cloned.1.call-done = bf16[6144,128]{1,0:T(8,128)(2,1)} async-done(((bf16[512,128]{1,0:T(8,128)(2,1)}), bf16[6144,128]{1,0:T(8,128)(2,1)}) %all-gather.3.cloned.1.call-update) | async-done | bytes 1572880 | tf_op jit(solution)/shard_map/all_gather | solution.py:59
  71.5 8.9 %collective-permute-start = (bf16[12,512,128]{2,1,0:T(8,128)(2,1)}, bf16[12,512,128]{2,1,0:T(8,128)(2,1)}, u32[]{:S(2)}, u32[]{:S(2)}) collective-permute-start(bf16[12,512,128]{2,1,0:T(8,128)(2,1)} %bitcast.17), channel_id=1, source_target_pairs={{0,32},{32,0},{1,33},{33,1},{2,34},{34,2},{3,35},{35,3},{4,36},{36... | collective-permute-start | bytes 4718600 | tf_op jit(solution)/shard_map/ppermute | solution.py:60
  81.1 0.0 copy-done.4
  81.1 0.0 copy-start.1
  81.1 0.0 copy-start.2
  81.1 0.0 copy-start.3
  81.1 1.3 copy.14
  82.5 1.3 multiply_bitcast_fusion.taper_ref
  83.8 0.0 all-to-all-done.1
  83.8 0.0 collective-permute-done.other_ref
  83.8 0.0 copy-done.1
  83.8 0.0 copy-done.2
  83.8 0.0 copy-done.3
  83.8 0.0 copy-start
  83.8 1.4 copy-done
  85.2 6.2 %pairs.1 = bf16[256,4096]{1,0:T(8,128)(2,1)S(1)} custom-call(s32[32]{0:T(128)S(1)} %bitcast.19, s32[32]{0:T(128)S(1)} %bitcast.20, s32[32]{0:T(128)S(1)} %bitcast.21, s32[1]{0:T(128)} %bitcast.14.count_ref, s32[1]{0:T(128)} %bitcast.4.core_ref, bf16[256,4096]{1,0:T(8,128)(2,1)S(1)} %bitcast.15, bf16[12,512,128]{2,1,0:T(8,128)(2,1)S(1)} %bitcast.18, ...), custom_call_target="tpu_custom_call" | custom-call | tf_op jit(solution)/shard_map/pairs/pallas_call | solution.py:68
  91.4 27.9 %all_to_all.21 = bf16[4,64,4096]{2,1,0:T(8,128)(2,1)S(1)} all-to-all(bf16[4,64,4096]{2,1,0:T(8,128)(2,1)S(1)} %bitcast.16), channel_id=1, replica_groups=mesh['z'=12,'core'=2,'x'=4,'y'=8] {'x'}, dimensions={0} | all-to-all | bytes 4194304 | tf_op jit(solution)/shard_map/all_to_all | solution.py:83
  119.3 0.0 copy-start.5
  119.3 0.4 reduce_sum.21
  119.7 24.5 %all_to_all.22 = bf16[8,8,4096]{2,1,0:T(8,128)(2,1)S(1)} all-to-all(bf16[8,8,4096]{2,1,0:T(8,128)(2,1)S(1)} %bitcast.23), channel_id=1, replica_groups=mesh['z'=12,'core'=2,'x'=4,'y'=8] {'y'}, dimensions={0} | all-to-all | bytes 1048576 | tf_op jit(solution)/shard_map/all_to_all | solution.py:85
  144.1 0.1 convert_reduce_fusion
  144.2 0.0 copy-done.5
  144.2 0.6 add_convert_fusion
Async XLA Ops:
  6.5 64.9 %all-gather.3.cloned.1.call-start = ((), (), s32[]{:S(2)}) async-start(), calls=%async_computation.4 | async-start | bytes 1703936 | tf_op jit(solution)/shard_map/all_gather | solution.py:59
  31.2 49.8 %copy-start.4 = (f32[16,128,128]{2,1,0:T(8,128)S(1)}, f32[16,128,128]{2,1,0:T(8,128)}, u32[]{:S(2)}) copy-start(f32[16,128,128]{2,1,0:T(8,128)} %param.11) | copy-start | bytes 3145732
  31.2 52.5 %all-to-all-start.1 = ((bf16[4,64,4096]{2,1,0:T(8,128)(2,1)}), bf16[4,64,4096]{2,1,0:T(8,128)(2,1)S(1)}, u32[]{:S(2)}, u32[]{:S(2)}) async-start(bf16[4,64,4096]{2,1,0:T(8,128)(2,1)} %broadcast_in_dim.15), calls=%async_computation.1 | async-start | bytes 4194304 | tf_op jit(solution)/shard_map/all_to_all | solution.py:63
  71.5 12.3 %collective-permute-start = (bf16[12,512,128]{2,1,0:T(8,128)(2,1)}, bf16[12,512,128]{2,1,0:T(8,128)(2,1)}, u32[]{:S(2)}, u32[]{:S(2)}) collective-permute-start(bf16[12,512,128]{2,1,0:T(8,128)(2,1)} %bitcast.17), channel_id=1, source_target_pairs={{0,32},{32,0},{1,33},{33,1},{2,34},{34,2},{3,35},{35,3},{4,36},{36... | collective-permute-start | bytes 4718600 | tf_op jit(solution)/shard_map/ppermute | solution.py:60
  81.1 2.7 %copy-start.1 = (s32[1,1,32]{2,1,0:T(1,128)S(1)}, s32[1,1,32]{2,1,0:T(1,128)}, u32[]{:S(2)}) copy-start(s32[1,1,32]{2,1,0:T(1,128)} %param.13) | copy-start | bytes 388
  81.1 2.7 %copy-start.2 = (s32[1,1,32]{2,1,0:T(1,128)S(1)}, s32[1,1,32]{2,1,0:T(1,128)}, u32[]{:S(2)}) copy-start(s32[1,1,32]{2,1,0:T(1,128)} %param.12) | copy-start | bytes 388
  81.1 2.7 %copy-start.3 = (s32[1,1,32]{2,1,0:T(1,128)S(1)}, s32[1,1,32]{2,1,0:T(1,128)}, u32[]{:S(2)}) copy-start(s32[1,1,32]{2,1,0:T(1,128)} %param.14) | copy-start | bytes 388
  83.8 1.4 copy-start
  119.3 24.9 %copy-start.5 = (bf16[8,4096]{1,0:T(8,128)(2,1)S(1)}, bf16[8,4096]{1,0:T(8,128)(2,1)}, u32[]{:S(2)}) copy-start(bf16[8,4096]{1,0:T(8,128)(2,1)} %param.8) | copy-start | bytes 196612
Sparse Core Ops, SparseCore 0:
  9.7 61.6 all-gather.2

commit v2 on v1

v2 whole, which is shorter than its diff:
```python
import jax
import jax.numpy as jnp
from jax import lax
from jax.experimental import pallas as pl
from jax.experimental.pallas import tpu as pltpu
from jax.sharding import Mesh, PartitionSpec as P

Z, CORE, X, YH, YL = 12, 2, 4, 4, 2
Y = YH * YL
UNROLL = 4


def anomaly_kernel(panel_ref, anom_ref):
    tiles, width, members = anom_ref.shape

    @pl.loop(0, tiles)
    def _(t):
        cells = panel_ref[:, pl.ds(pl.multiple_of(t * width, width), width)].astype(jnp.float32)
        centre = jnp.sum(cells, axis=0, keepdims=True) * (1.0 / members)
        anom_ref[t] = (cells - centre).T.astype(jnp.bfloat16)


def pair_kernel(
    tile_ref, obs_ref, kind_ref, count_ref, anom_ref, blocks_ref, taper_ref, out_ref, acc_ref
):
    tiles, members, width = acc_ref.shape

    @pl.loop(0, tiles)
    def _(t):
        acc_ref[t] = jnp.zeros((members, width), jnp.float32)

    count = count_ref[0]

    @pl.loop(0, lax.div(count + (UNROLL - 1), UNROLL))
    def _(step):
        terms = []
        for u in range(UNROLL):
            q = step * UNROLL + u
            t, j, k = tile_ref[q], obs_ref[q], kind_ref[q]
            cross = jnp.dot(
                anom_ref[t], blocks_ref[j, 0:members], preferred_element_type=jnp.float32
            )
            scaled = taper_ref[k] * cross * (1.0 / (members - 1))
            gain = jnp.where(q < count, scaled, 0.0).astype(jnp.bfloat16)
            term = lax.dot_general(
                blocks_ref[j, members : 2 * members],
                gain,
                (((1,), (1,)), ((), ())),
                preferred_element_type=jnp.float32,
            )
            terms.append((t, term))
        for t, term in terms:
            acc_ref[t] += term

    @pl.loop(0, tiles)
    def _(t):
        out_ref[:, pl.ds(pl.multiple_of(t * width, width), width)] = acc_ref[t].astype(jnp.bfloat16)


def on_device(
    ensemble, obs_anom, obs_weight, taper_table, pair_obs, pair_tile, pair_taper, pair_count
):
    rows, cells = ensemble.shape
    members = rows * X * Y
    width = obs_anom.shape[1]
    tiles = cells // width
    weight = obs_weight.reshape(X, YH, YL, rows, width).transpose(0, 2, 1, 3, 4)
    blocks = jnp.concatenate([obs_anom, weight.reshape(members, width)], axis=0)
    blocks = lax.all_gather(blocks, ("z", "core"), axis=0)
    y_axes = ("yh", "yl")
    part = lax.all_to_all(
        jnp.broadcast_to(ensemble[None], (Y, rows, cells)), y_axes, 0, 0, tiled=True
    )
    part = part.reshape(1, Y * rows, cells)
    panel = lax.all_to_all(jnp.broadcast_to(part, (X, Y * rows, cells)), "x", 0, 0, tiled=True)
    smem = pl.BlockSpec(memory_space=pltpu.SMEM)
    vmem = pl.BlockSpec(memory_space=pltpu.VMEM)
    anom = pl.pallas_call(
        anomaly_kernel,
        out_shape=jax.ShapeDtypeStruct((tiles, width, members), jnp.bfloat16),
        in_specs=[vmem],
        out_specs=vmem,
        compiler_params=pltpu.CompilerParams(vmem_limit_bytes=24 * 2**20),
        name="anomalies",
    )(panel.reshape(members, cells))
    partial = pl.pallas_call(
        pair_kernel,
        out_shape=jax.ShapeDtypeStruct((members, cells), jnp.bfloat16),
        in_specs=[smem] * 4 + [vmem] * 3,
        out_specs=vmem,
        scratch_shapes=[pltpu.VMEM((tiles, members, width), jnp.float32)],
        compiler_params=pltpu.CompilerParams(vmem_limit_bytes=40 * 2**20),
        name="pairs",
    )(pair_tile[0, 0], pair_obs[0, 0], pair_taper[0, 0], pair_count[0], anom, blocks, taper_table)
    sent = partial.reshape(X * YL, YH * rows, cells)
    sent = lax.all_to_all(sent, ("x", "yl"), 0, 0, tiled=True)
    summed = jnp.sum(sent.astype(jnp.float32), axis=0).astype(jnp.bfloat16)
    sent = lax.all_to_all(summed.reshape(YH, rows, cells), "yh", 0, 0, tiled=True)
    update = jnp.sum(sent.astype(jnp.float32), axis=0)
    return (ensemble.astype(jnp.float32) + update).astype(jnp.bfloat16)


def solution(mesh):
    fine = Mesh(
        mesh.devices.reshape(Z, CORE, X, YH, YL), ("z", "core", "x", "yh", "yl")
    )
    group, route = ("z", "core"), ("x", "yh", "yl")
    placed = (
        P(route, group),
        P(None, group + route),
        P(None, group + route),
        P(),
        P(group, route, None),
        P(group, route, None),
        P(group, route, None),
        P(group, route),
    )
    return jax.shard_map(
        on_device, mesh=fine, in_specs=placed, out_specs=P(route, group), check_vma=False
    )
```

time: 153 us -> 140 us (0.915)
  starting transfers between devices: 16.8 us -> 7.8 us
  blocking collectives: 72 us -> 66.2 us
  Pallas kernels: 6.18 us -> 8.97 us
  local copies, waits for them, and re-layouts: 6.27 us -> 8.16 us
    all_gather x1, waiting for transfers between devices: 32.3 us -> 9.01 us  [on_device(): blocks = lax.all_gather(blocks, ('z', 'core'), axis=0)]
    all_to_all x1, waiting for transfers between devices: 0.01 us -> 23 us  [on_device(): lax.all_to_all(jnp.broadcast_to(part, (X, Y * rows, cells)), 'x', 0, 0, t...]
    ppermute x1 -> x0, starting transfers between devices: 8.92 us -> none  [on_device(): other = lax.ppermute(own, 'core', [(0, 1), (1, 0)])]
    all_to_all x3, blocking collectives: 72 us -> 66.2 us  [the longest x1 30.4 us: on_device(): sent = lax.all_to_all(sent, ('x', 'yl'), 0, 0, tiled=True)]
    pallas_call x0 -> x1, Pallas kernels: none -> 4.66 us  [on_device(): pl.pallas_call(anomaly_kernel, out_shape=jax.ShapeDtypeStruct((tiles, wid...]
    pallas_call x1, Pallas kernels: 6.18 us -> 4.31 us  [on_device(): pl.pallas_call(pair_kernel, out_shape=jax.ShapeDtypeStruct((members, cell...]
    unnamed x15 -> x16, local copies, waits for them, and re-layouts: 3.01 us -> 4.84 us
  transfers between devices with their start and end apart: 3 -> 2, of which waited for: 1 -> 2; matrix products, arithmetic and copies ran while one was open for 3% -> 2% of each run, Pallas kernels for 0% -> 3%
where the time goes in v2:
time: 140 us
  blocking collectives  66.2 us (47%)
  waiting for transfers between devices  32 us (23%)
  between operations  14.1 us (10%)
  Pallas kernels  8.97 us (6%)
  local copies, waits for them, and re-layouts  8.16 us (6%)
  starting transfers between devices  7.8 us (6%)
  other arithmetic  2.53 us (2%)
    all_to_all x1, blocking collectives, on_device(): sent = lax.all_to_all(sent, ('x', 'yl'), 0, 0, tiled=True)  30.4 us
    all_to_all x1, waiting for transfers between devices, on_device(): lax.all_to_all(jnp.broadcast_to(part, (X, Y * rows, cells)), 'x', 0, 0, t...  23 us
    all_to_all x1, blocking collectives, on_device(): lax.all_to_all(jnp.broadcast_to(ensemble[None], (Y, rows, cells)), y_axes...  19.7 us
    all_to_all x1, blocking collectives, on_device(): lax.all_to_all(summed.reshape(YH, rows, cells), 'yh', 0, 0, tiled=True)  16.2 us
    all_gather x1, waiting for transfers between devices, on_device(): blocks = lax.all_gather(blocks, ('z', 'core'), axis=0)  9.01 us
    all_to_all x1, starting transfers between devices, on_device(): lax.all_to_all(jnp.broadcast_to(part, (X, Y * rows, cells)), 'x', 0, 0, t...  7.8 us
    unnamed x16, local copies, waits for them, and re-layouts  4.84 us
    pallas_call x1, Pallas kernels, on_device(): pl.pallas_call(anomaly_kernel, out_shape=jax.ShapeDtypeStruct((tiles, wid...  4.66 us
  transfers between devices with their start and end apart: 2, of which 2 were waited for; matrix products, arithmetic and copies ran while one was open for 2% of the time, Pallas kernels for 3%

profile of v2, /device:TPU:1, one launch (start us, length us, event | category | flops | bytes accessed | tf_op | source)
XLA Modules:
  0.0 139.7 jit_solution(5497016361578233450)
XLA Ops:
  6.5 0.0 all-gather.3.cloned.1.call-start
  6.5 0.8 copy.10
  7.4 1.5 %pad_maximum_fusion = bf16[512,128]{1,0:T(8,128)(2,1)} fusion(bf16[256,128]{1,0:T(8,128)(2,1)S(1)} %bitcast.22, bf16[256,128]{1,0:T(8,128)(2,1)} %param.9), kind=kLoop, calls=%fused_computation.1 | loop fusion | flops 262144 | bytes 262144 | tf_op jit(solution)/shard_map/concatenate | solution.py:68
  8.9 0.0 all-gather.3.cloned.1.call-update
  8.9 0.9 broadcast_in_dim.6
  9.8 19.7 %all_to_all.20 = bf16[8,8,4096]{2,1,0:T(8,128)(2,1)S(1)} all-to-all(bf16[8,8,4096]{2,1,0:T(8,128)(2,1)S(1)} %broadcast_in_dim.6), channel_id=1, replica_groups=mesh['z'=12,'core'=2,'x'=4,'yh'=4,'yl'=2] {'yh','yl'}, dimensions={0} | all-to-all | bytes 1048576 | tf_op jit(solution)/shard_map/all_to_all | solution.py:71
  29.5 1.6 %broadcast_in_dim.15 = bf16[4,64,4096]{2,1,0:T(8,128)(2,1)} broadcast(bf16[64,4096]{1,0:T(8,128)(2,1)S(1)} %bitcast.20), dimensions={1,2} | broadcast | bytes 2621440 | tf_op jit(solution)/shard_map/broadcast_in_dim | solution.py:75
  31.0 7.8 %all-to-all-start.1 = ((bf16[4,64,4096]{2,1,0:T(8,128)(2,1)}), bf16[4,64,4096]{2,1,0:T(8,128)(2,1)S(1)}, u32[]{:S(2)}, u32[]{:S(2)}) async-start(bf16[4,64,4096]{2,1,0:T(8,128)(2,1)} %broadcast_in_dim.15), calls=%async_computation.1 | async-start | bytes 4194304 | tf_op jit(solution)/shard_map/all_to_all | solution.py:75
  39.5 23.0 %all-to-all-done.1 = bf16[4,64,4096]{2,1,0:T(8,128)(2,1)S(1)} async-done(((bf16[4,64,4096]{2,1,0:T(8,128)(2,1)}), bf16[4,64,4096]{2,1,0:T(8,128)(2,1)S(1)}, u32[]{:S(2)}, u32[]{:S(2)}) %all-to-all-start.1) | async-done | bytes 2097184 | tf_op jit(solution)/shard_map/all_to_all | solution.py:75
  62.5 0.0 copy-start
  62.5 1.3 copy-done
  63.8 0.0 copy-start.1
  63.8 1.6 %copy-done.1 = bf16[4,64,4096]{2,1,0:T(8,128)(2,1)S(1)} copy-done((bf16[4,64,4096]{2,1,0:T(8,128)(2,1)S(1)}, bf16[4,64,4096]{2,1,0:T(8,128)(2,1)}, u32[]{:S(2)}) %copy-start.1) | copy-done | bytes 2097176
  65.4 0.0 copy-start.3
  65.4 0.0 copy-start.4
  65.4 0.0 copy-start.5
  65.4 0.0 copy-start.6
  65.4 4.7 %anomalies.1.anom_ref = bf16[32,128,256]{2,1,0:T(8,128)(2,1)S(1)} custom-call(bf16[256,4096]{1,0:T(8,128)(2,1)S(1)} %bitcast.15), custom_call_target="tpu_custom_call" | custom-call | tf_op jit(solution)/shard_map/anomalies/pallas_call | solution.py:78
  70.1 9.0 %all-gather.3.cloned.1.call-done = bf16[12288,128]{1,0:T(8,128)(2,1)} async-done(((bf16[512,128]{1,0:T(8,128)(2,1)}), bf16[12288,128]{1,0:T(8,128)(2,1)}) %all-gather.3.cloned.1.call-update) | async-done | bytes 3145744 | tf_op jit(solution)/shard_map/all_gather | solution.py:69
  79.1 0.0 copy-done.3
  79.1 0.0 copy-done.4
  79.1 0.0 copy-done.5
  79.1 0.0 copy-done.6
  79.1 0.0 copy-start.2
  79.1 1.9 %copy-done.2 = bf16[12288,128]{1,0:T(8,128)(2,1)S(1)} copy-done((bf16[12288,128]{1,0:T(8,128)(2,1)S(1)}, bf16[12288,128]{1,0:T(8,128)(2,1)}, u32[]{:S(2)}) %copy-start.2) | copy-done | bytes 3145752
  81.0 4.3 %pairs.1 = bf16[256,4096]{1,0:T(8,128)(2,1)S(1)} custom-call(s32[32]{0:T(128)S(1)} %bitcast.17, s32[32]{0:T(128)S(1)} %bitcast.18, s32[32]{0:T(128)S(1)} %bitcast.19, s32[1]{0:T(128)} %bitcast.13.count_ref, bf16[32,128,256]{2,1,0:T(8,128)(2,1)S(1)} %anomalies.1.anom_ref, bf16[24,512,128]{2,1,0:T(8,128)(2,1)S(1)} %bitcast.16, f32[16,128,128]{2,1,0:T(8,128)S(1)} %copy-done.3), custom_call_target="tpu_custom_call" | custom-call | tf_op jit(solution)/shard_map/pairs/pallas_call | solution.py:86
  85.3 30.4 %all_to_all.21 = bf16[8,32,4096]{2,1,0:T(8,128)(2,1)S(1)} all-to-all(bf16[8,32,4096]{2,1,0:T(8,128)(2,1)S(1)} %bitcast.14), channel_id=1, replica_groups=mesh['z'=12,'core'=2,'x'=4,'yh'=4,'yl'=2] {'x','yl'}, dimensions={0} | all-to-all | bytes 4194304 | tf_op jit(solution)/shard_map/all_to_all | solution.py:96
  115.7 0.0 copy-start.7
  115.7 0.3 reduce_sum.21
  116.0 16.2 %all_to_all.22 = bf16[4,8,4096]{2,1,0:T(8,128)(2,1)S(1)} all-to-all(bf16[4,8,4096]{2,1,0:T(8,128)(2,1)S(1)} %bitcast.21), channel_id=1, replica_groups=mesh['z'=12,'core'=2,'x'=4,'yh'=4,'yl'=2] {'yh'}, dimensions={0} | all-to-all | bytes 524288 | tf_op jit(solution)/shard_map/all_to_all | solution.py:98
  132.2 0.0 copy-done.7
  132.2 0.7 add_convert_fusion
  (1 shorter events, 0.0 us)
Async XLA Ops:
  6.5 72.6 %all-gather.3.cloned.1.call-start = ((), (), s32[]{:S(2)}) async-start(), calls=%async_computation.4 | async-start | bytes 3276800 | tf_op jit(solution)/shard_map/all_gather | solution.py:69
  31.0 31.4 %all-to-all-start.1 = ((bf16[4,64,4096]{2,1,0:T(8,128)(2,1)}), bf16[4,64,4096]{2,1,0:T(8,128)(2,1)S(1)}, u32[]{:S(2)}, u32[]{:S(2)}) async-start(bf16[4,64,4096]{2,1,0:T(8,128)(2,1)} %broadcast_in_dim.15), calls=%async_computation.1 | async-start | bytes 4194304 | tf_op jit(solution)/shard_map/all_to_all | solution.py:75
  62.5 1.4 copy-start
  63.8 1.6 %copy-start.1 = (bf16[4,64,4096]{2,1,0:T(8,128)(2,1)S(1)}, bf16[4,64,4096]{2,1,0:T(8,128)(2,1)}, u32[]{:S(2)}) copy-start(bf16[4,64,4096]{2,1,0:T(8,128)(2,1)} %copy-done) | copy-start | bytes 6291460
  65.4 13.7 %copy-start.3 = (f32[16,128,128]{2,1,0:T(8,128)S(1)}, f32[16,128,128]{2,1,0:T(8,128)}, u32[]{:S(2)}) copy-start(f32[16,128,128]{2,1,0:T(8,128)} %taper_ref.1) | copy-start | bytes 3145732
  65.4 13.7 %copy-start.4 = (s32[1,1,32]{2,1,0:T(1,128)S(1)}, s32[1,1,32]{2,1,0:T(1,128)}, u32[]{:S(2)}) copy-start(s32[1,1,32]{2,1,0:T(1,128)} %param.13) | copy-start | bytes 388
  65.4 13.7 %copy-start.5 = (s32[1,1,32]{2,1,0:T(1,128)S(1)}, s32[1,1,32]{2,1,0:T(1,128)}, u32[]{:S(2)}) copy-start(s32[1,1,32]{2,1,0:T(1,128)} %param.12) | copy-start | bytes 388
  65.4 13.7 %copy-start.6 = (s32[1,1,32]{2,1,0:T(1,128)S(1)}, s32[1,1,32]{2,1,0:T(1,128)}, u32[]{:S(2)}) copy-start(s32[1,1,32]{2,1,0:T(1,128)} %param.14) | copy-start | bytes 388
  79.1 1.9 %copy-start.2 = (bf16[12288,128]{1,0:T(8,128)(2,1)S(1)}, bf16[12288,128]{1,0:T(8,128)(2,1)}, u32[]{:S(2)}) copy-start(bf16[12288,128]{1,0:T(8,128)(2,1)} %all-gather.3.cloned.1.call-done) | copy-start | bytes 9437188
  115.7 16.6 %copy-start.7 = (bf16[8,4096]{1,0:T(8,128)(2,1)S(1)}, bf16[8,4096]{1,0:T(8,128)(2,1)}, u32[]{:S(2)}) copy-start(bf16[8,4096]{1,0:T(8,128)(2,1)} %param.8) | copy-start | bytes 196612
Sparse Core Ops, SparseCore 0:
  9.8 69.2 all-gather.2

commit v3 on v2

v3 whole, which is shorter than its diff:
```python
import jax
import jax.numpy as jnp
from jax import lax
from jax.experimental import pallas as pl
from jax.experimental.pallas import tpu as pltpu
from jax.sharding import Mesh, PartitionSpec as P

Z, CORE, X, YH, YL = 12, 2, 4, 4, 2
Y = YH * YL
UNROLL = 4


def anomaly_kernel(panel_ref, anom_ref):
    tiles, members, width = anom_ref.shape

    @pl.loop(0, tiles, unroll=2)
    def _(t):
        cells = panel_ref[:, pl.ds(pl.multiple_of(t * width, width), width)].astype(jnp.float32)
        centre = jnp.sum(cells, axis=0, keepdims=True) * (1.0 / members)
        anom_ref[t] = (cells - centre).astype(jnp.bfloat16)


def pair_kernel(
    tile_ref, obs_ref, kind_ref, count_ref, anom_ref, blocks_ref, taper_ref, out_ref,
    acc_ref, held_ref, sems,
):
    tiles, members, width = acc_ref.shape
    count = count_ref[0]
    steps = lax.div(count + (UNROLL - 1), UNROLL)

    def fetch(q):
        return pltpu.make_async_copy(blocks_ref.at[obs_ref[q]], held_ref.at[q], sems.at[q])

    @pl.loop(0, steps * UNROLL)
    def _(q):
        fetch(q).start()

    @pl.loop(0, tiles)
    def _(t):
        acc_ref[t] = jnp.zeros((members, width), jnp.float32)

    @pl.loop(0, steps)
    def _(step):
        for u in range(UNROLL):
            fetch(step * UNROLL + u).wait()
        terms = []
        for u in range(UNROLL):
            q = step * UNROLL + u
            t, k = tile_ref[q], kind_ref[q]
            y = jnp.concatenate([held_ref[q, 0:128], held_ref[q, 128:256]], axis=1)
            cross = jnp.dot(y, anom_ref[t], preferred_element_type=jnp.float32)
            gain = jnp.where(q < count, taper_ref[k] * cross, 0.0).astype(jnp.bfloat16)
            w = held_ref[q, members : 2 * members]
            terms.append((t, jnp.dot(w, gain, preferred_element_type=jnp.float32)))
        for t, term in terms:
            acc_ref[t] += term

    @pl.loop(0, tiles, unroll=2)
    def _(t):
        out_ref[:, pl.ds(pl.multiple_of(t * width, width), width)] = acc_ref[t].astype(jnp.bfloat16)


def on_device(
    ensemble, obs_anom, obs_weight, taper_table, pair_obs, pair_tile, pair_taper, pair_count
):
    rows, cells = ensemble.shape
    members = rows * X * Y
    width = obs_anom.shape[1]
    tiles = cells // width
    pairs = pair_tile.shape[2]
    half = members // 2
    weight = obs_weight.reshape(X, YH, YL, rows, width).transpose(0, 2, 1, 3, 4)
    blocks = jnp.concatenate(
        [obs_anom[:half].T, obs_anom[half:].T, weight.reshape(members, width)], axis=0
    )
    blocks = lax.all_gather(blocks, ("z", "core"), axis=0)
    y_axes = ("yh", "yl")
    part = lax.all_to_all(
        jnp.broadcast_to(ensemble[None], (Y, rows, cells)), y_axes, 0, 0, tiled=True
    )
    part = part.reshape(1, Y * rows, cells)
    panel = lax.all_to_all(jnp.broadcast_to(part, (X, Y * rows, cells)), "x", 0, 0, tiled=True)
    tapers = jnp.swapaxes(taper_table, 1, 2) * (1.0 / (members - 1))
    smem = pl.BlockSpec(memory_space=pltpu.SMEM)
    vmem = pl.BlockSpec(memory_space=pltpu.VMEM)
    anom = pl.pallas_call(
        anomaly_kernel,
        out_shape=jax.ShapeDtypeStruct((tiles, members, width), jnp.bfloat16),
        in_specs=[vmem],
        out_specs=vmem,
        compiler_params=pltpu.CompilerParams(vmem_limit_bytes=10 * 2**20),
        name="anomalies",
    )(panel.reshape(members, cells))
    partial = pl.pallas_call(
        pair_kernel,
        out_shape=jax.ShapeDtypeStruct((members, cells), jnp.bfloat16),
        in_specs=[smem] * 4 + [vmem, pl.BlockSpec(memory_space=pltpu.HBM), vmem],
        out_specs=vmem,
        scratch_shapes=[
            pltpu.VMEM((tiles, members, width), jnp.float32),
            pltpu.VMEM((pairs, 2 * members, width), jnp.bfloat16),
            pltpu.SemaphoreType.DMA((pairs,)),
        ],
        compiler_params=pltpu.CompilerParams(vmem_limit_bytes=47 * 2**20),
        name="pairs",
    )(pair_tile[0, 0], pair_obs[0, 0], pair_taper[0, 0], pair_count[0], anom, blocks, tapers)
    sent = partial.reshape(X * YL, YH * rows, cells)
    sent = lax.all_to_all(sent, ("x", "yl"), 0, 0, tiled=True)
    summed = jnp.sum(sent.astype(jnp.float32), axis=0).astype(jnp.bfloat16)
    sent = lax.all_to_all(summed.reshape(YH, rows, cells), "yh", 0, 0, tiled=True)
    update = jnp.sum(sent.astype(jnp.float32), axis=0)
    return (ensemble.astype(jnp.float32) + update).astype(jnp.bfloat16)


def solution(mesh):
    fine = Mesh(
        mesh.devices.reshape(Z, CORE, X, YH, YL), ("z", "core", "x", "yh", "yl")
    )
    group, route = ("z", "core"), ("x", "yh", "yl")
    placed = (
        P(route, group),
        P(None, group + route),
        P(None, group + route),
        P(),
        P(group, route, None),
        P(group, route, None),
        P(group, route, None),
        P(group, route),
    )
    return jax.shard_map(
        on_device, mesh=fine, in_specs=placed, out_specs=P(route, group), check_vma=False
    )
```

time: 140 us -> 140 us (level); the launches traced: 140 us -> 138 us
  Pallas kernels: 8.97 us -> 6.53 us
    pallas_call x1, Pallas kernels: 4.66 us -> 1.06 us  [on_device(): pl.pallas_call(anomaly_kernel, out_shape=jax.ShapeDtypeStruct((tiles, mem...]
    all_gather x1, waiting for transfers between devices: 9.01 us -> 12.3 us  [on_device(): blocks = lax.all_gather(blocks, ('z', 'core'), axis=0)]
    all_to_all x1, waiting for transfers between devices: 23 us -> 20.3 us  [on_device(): lax.all_to_all(jnp.broadcast_to(part, (X, Y * rows, cells)), 'x', 0, 0, t...]
    all_to_all x1, blocking collectives: 16.2 us -> 14.7 us  [on_device(): lax.all_to_all(summed.reshape(YH, rows, cells), 'yh', 0, 0, tiled=True)]
    unnamed x16 -> x15, local copies, waits for them, and re-layouts: 4.84 us -> 4.32 us
  transfers between devices with their start and end apart: 2 -> 2, of which waited for: 2 -> 2; matrix products, arithmetic and copies ran while one was open for 2% -> 4% of each run, Pallas kernels for 3% -> 1%
where the time goes in v3:
time: 140 us; the launch traced here: 138 us
  blocking collectives  65.1 us (46%)
  waiting for transfers between devices  32.6 us (23%)
  between operations  14.1 us (10%)
  local copies, waits for them, and re-layouts  8.66 us (6%)
  starting transfers between devices  7.93 us (6%)
  Pallas kernels  6.53 us (5%)
  other arithmetic  3.01 us (2%)
    all_to_all x1, blocking collectives, on_device(): sent = lax.all_to_all(sent, ('x', 'yl'), 0, 0, tiled=True)  30.7 us
    all_to_all x1, waiting for transfers between devices, on_device(): lax.all_to_all(jnp.broadcast_to(part, (X, Y * rows, cells)), 'x', 0, 0, t...  20.3 us
    all_to_all x1, blocking collectives, on_device(): lax.all_to_all(jnp.broadcast_to(ensemble[None], (Y, rows, cells)), y_axes...  19.7 us
    all_to_all x1, blocking collectives, on_device(): lax.all_to_all(summed.reshape(YH, rows, cells), 'yh', 0, 0, tiled=True)  14.7 us
    all_gather x1, waiting for transfers between devices, on_device(): blocks = lax.all_gather(blocks, ('z', 'core'), axis=0)  12.3 us
    all_to_all x1, starting transfers between devices, on_device(): lax.all_to_all(jnp.broadcast_to(part, (X, Y * rows, cells)), 'x', 0, 0, t...  7.93 us
    pallas_call x1, Pallas kernels, on_device(): pl.pallas_call(pair_kernel, out_shape=jax.ShapeDtypeStruct((members, cell...  5.47 us
    unnamed x15, local copies, waits for them, and re-layouts  4.32 us
  transfers between devices with their start and end apart: 2, of which 2 were waited for; matrix products, arithmetic and copies ran while one was open for 4% of the time, Pallas kernels for 1%

profile of v3, /device:TPU:1, one launch (start us, length us, event | category | flops | bytes accessed | tf_op | source)
XLA Modules:
  0.0 137.9 jit_solution(2966178757650815624)
XLA Ops:
  6.5 0.0 all-gather.3.cloned.1.call-start
  6.5 0.8 slice_bitcast_fusion.1
  7.3 0.1 copy.14
  7.4 0.1 copy.15
  7.6 0.9 copy.13
  8.4 0.7 pad_maximum_fusion
  9.1 0.0 all-gather.3.cloned.1.call-update
  9.1 0.9 broadcast_in_dim.6
  10.0 19.7 %all_to_all.20 = bf16[8,8,4096]{2,1,0:T(8,128)(2,1)S(1)} all-to-all(bf16[8,8,4096]{2,1,0:T(8,128)(2,1)S(1)} %broadcast_in_dim.6), channel_id=1, replica_groups=mesh['z'=12,'core'=2,'x'=4,'yh'=4,'yl'=2] {'yh','yl'}, dimensions={0} | all-to-all | bytes 1048576 | tf_op jit(solution)/shard_map/all_to_all | solution.py:78
  29.6 1.6 %broadcast_in_dim.15 = bf16[4,64,4096]{2,1,0:T(8,128)(2,1)} broadcast(bf16[64,4096]{1,0:T(8,128)(2,1)S(1)} %bitcast.26), dimensions={1,2} | broadcast | bytes 2621440 | tf_op jit(solution)/shard_map/broadcast_in_dim | solution.py:82
  31.2 0.0 copy-start.5
  31.2 7.9 %all-to-all-start.1 = ((bf16[4,64,4096]{2,1,0:T(8,128)(2,1)}), bf16[4,64,4096]{2,1,0:T(8,128)(2,1)S(1)}, u32[]{:S(2)}, u32[]{:S(2)}) async-start(bf16[4,64,4096]{2,1,0:T(8,128)(2,1)} %broadcast_in_dim.15), calls=%async_computation.1 | async-start | bytes 4194304 | tf_op jit(solution)/shard_map/all_to_all | solution.py:82
  39.2 0.0 copy-done.5
  39.2 1.3 copy.16
  41.2 1.3 multiply_bitcast_fusion.taper_ref
  42.5 20.3 %all-to-all-done.1 = bf16[4,64,4096]{2,1,0:T(8,128)(2,1)S(1)} async-done(((bf16[4,64,4096]{2,1,0:T(8,128)(2,1)}), bf16[4,64,4096]{2,1,0:T(8,128)(2,1)S(1)}, u32[]{:S(2)}, u32[]{:S(2)}) %all-to-all-start.1) | async-done | bytes 2097184 | tf_op jit(solution)/shard_map/all_to_all | solution.py:82
  62.8 0.0 copy-start
  62.8 1.3 copy-done
  64.1 0.0 copy-start.1
  64.1 1.6 %copy-done.1 = bf16[4,64,4096]{2,1,0:T(8,128)(2,1)S(1)} copy-done((bf16[4,64,4096]{2,1,0:T(8,128)(2,1)S(1)}, bf16[4,64,4096]{2,1,0:T(8,128)(2,1)}, u32[]{:S(2)}) %copy-start.1) | copy-done | bytes 2097176
  65.8 0.0 copy-start.2
  65.8 0.0 copy-start.3
  65.8 0.0 copy-start.4
  65.8 1.1 anomalies.1.anom_ref
  66.8 12.3 %all-gather.3.cloned.1.call-done = bf16[12288,128]{1,0:T(8,128)(2,1)} async-done(((bf16[512,128]{1,0:T(8,128)(2,1)}), bf16[12288,128]{1,0:T(8,128)(2,1)}) %all-gather.3.cloned.1.call-update) | async-done | bytes 3145744 | tf_op jit(solution)/shard_map/all_gather | solution.py:76
  79.1 0.0 copy-done.2
  79.1 0.0 copy-done.3
  79.1 0.0 copy-done.4
  79.1 5.5 %pairs.1 = bf16[256,4096]{1,0:T(8,128)(2,1)S(1)} custom-call(s32[32]{0:T(128)S(1)} %bitcast.22, s32[32]{0:T(128)S(1)} %bitcast.23, s32[32]{0:T(128)S(1)} %bitcast.24, s32[1]{0:T(128)} %bitcast.19.count_ref, bf16[32,256,128]{2,1,0:T(8,128)(2,1)S(1)} %anomalies.1.anom_ref, bf16[24,512,128]{2,1,0:T(8,128)(2,1)} %bitcast.25, ...), custom_call_target="tpu_custom_call" | custom-call | tf_op jit(solution)/shard_map/pairs/pallas_call | solution.py:94
  84.6 30.7 %all_to_all.21 = bf16[8,32,4096]{2,1,0:T(8,128)(2,1)S(1)} all-to-all(bf16[8,32,4096]{2,1,0:T(8,128)(2,1)S(1)} %bitcast.20), channel_id=1, replica_groups=mesh['z'=12,'core'=2,'x'=4,'yh'=4,'yl'=2] {'x','yl'}, dimensions={0} | all-to-all | bytes 4194304 | tf_op jit(solution)/shard_map/all_to_all | solution.py:108
  115.3 0.0 copy-start.6
  115.3 0.3 reduce_sum.21
  115.6 14.7 %all_to_all.22 = bf16[4,8,4096]{2,1,0:T(8,128)(2,1)S(1)} all-to-all(bf16[4,8,4096]{2,1,0:T(8,128)(2,1)S(1)} %bitcast.27), channel_id=1, replica_groups=mesh['z'=12,'core'=2,'x'=4,'yh'=4,'yl'=2] {'yh'}, dimensions={0} | all-to-all | bytes 524288 | tf_op jit(solution)/shard_map/all_to_all | solution.py:110
  130.3 0.0 copy-done.6
  130.4 0.7 add_convert_fusion
  (1 shorter events, 0.0 us)
Async XLA Ops:
  6.5 72.5 %all-gather.3.cloned.1.call-start = ((), (), s32[]{:S(2)}) async-start(), calls=%async_computation.4 | async-start | bytes 3276800 | tf_op jit(solution)/shard_map/all_gather | solution.py:76
  31.2 7.9 %copy-start.5 = (f32[16,128,128]{2,1,0:T(8,128)S(1)}, f32[16,128,128]{2,1,0:T(8,128)}, u32[]{:S(2)}) copy-start(f32[16,128,128]{2,1,0:T(8,128)} %param.11) | copy-start | bytes 3145732
  31.2 31.6 %all-to-all-start.1 = ((bf16[4,64,4096]{2,1,0:T(8,128)(2,1)}), bf16[4,64,4096]{2,1,0:T(8,128)(2,1)S(1)}, u32[]{:S(2)}, u32[]{:S(2)}) async-start(bf16[4,64,4096]{2,1,0:T(8,128)(2,1)} %broadcast_in_dim.15), calls=%async_computation.1 | async-start | bytes 4194304 | tf_op jit(solution)/shard_map/all_to_all | solution.py:82
  62.8 1.4 copy-start
  64.1 1.6 %copy-start.1 = (bf16[4,64,4096]{2,1,0:T(8,128)(2,1)S(1)}, bf16[4,64,4096]{2,1,0:T(8,128)(2,1)}, u32[]{:S(2)}) copy-start(bf16[4,64,4096]{2,1,0:T(8,128)(2,1)} %copy-done) | copy-start | bytes 6291460
  65.8 13.3 %copy-start.2 = (s32[1,1,32]{2,1,0:T(1,128)S(1)}, s32[1,1,32]{2,1,0:T(1,128)}, u32[]{:S(2)}) copy-start(s32[1,1,32]{2,1,0:T(1,128)} %param.13) | copy-start | bytes 388
  65.8 13.3 %copy-start.3 = (s32[1,1,32]{2,1,0:T(1,128)S(1)}, s32[1,1,32]{2,1,0:T(1,128)}, u32[]{:S(2)}) copy-start(s32[1,1,32]{2,1,0:T(1,128)} %param.12) | copy-start | bytes 388
  65.8 13.3 %copy-start.4 = (s32[1,1,32]{2,1,0:T(1,128)S(1)}, s32[1,1,32]{2,1,0:T(1,128)}, u32[]{:S(2)}) copy-start(s32[1,1,32]{2,1,0:T(1,128)} %param.14) | copy-start | bytes 388
  115.3 15.1 %copy-start.6 = (bf16[8,4096]{1,0:T(8,128)(2,1)S(1)}, bf16[8,4096]{1,0:T(8,128)(2,1)}, u32[]{:S(2)}) copy-start(bf16[8,4096]{1,0:T(8,128)(2,1)} %param.8) | copy-start | bytes 196612
Sparse Core Ops, SparseCore 0:
  9.8 69.2 all-gather.2

commit v4 on v3

--- a/solution.py
+++ b/solution.py
@@ -7,7 +7,7 @@
 
 Z, CORE, X, YH, YL = 12, 2, 4, 4, 2
 Y = YH * YL
-UNROLL = 4
+UNROLL = 16
 
 
 def anomaly_kernel(panel_ref, anom_ref):
@@ -22,40 +22,46 @@
 
 def pair_kernel(
     tile_ref, obs_ref, kind_ref, count_ref, anom_ref, blocks_ref, taper_ref, out_ref,
-    acc_ref, held_ref, sems,
+    acc_ref, held_ref, sems, gain_ref,
 ):
     tiles, members, width = acc_ref.shape
     count = count_ref[0]
     steps = lax.div(count + (UNROLL - 1), UNROLL)
 
-    def fetch(q):
-        return pltpu.make_async_copy(blocks_ref.at[obs_ref[q]], held_ref.at[q], sems.at[q])
+    y_copy = pltpu.make_async_copy(
+        blocks_ref.at[:, 0:members], held_ref.at[:, 0:members], sems.at[0]
+    )
+    w_copy = pltpu.make_async_copy(
+        blocks_ref.at[:, members : 2 * members], held_ref.at[:, members : 2 * members], sems.at[1]
+    )
+    y_copy.start()
+    w_copy.start()
 
-    @pl.loop(0, steps * UNROLL)
-    def _(q):
-        fetch(q).start()
-
-    @pl.loop(0, tiles)
+    @pl.loop(0, tiles, unroll=4)
     def _(t):
         acc_ref[t] = jnp.zeros((members, width), jnp.float32)
+
+    y_copy.wait()
 
     @pl.loop(0, steps)
     def _(step):
         for u in range(UNROLL):
-            fetch(step * UNROLL + u).wait()
-        terms = []
+            q = step * UNROLL + u
+            y = jnp.concatenate([held_ref[obs_ref[q], 0:128], held_ref[obs_ref[q], 128:256]], axis=1)
+            cross = jnp.dot(y, anom_ref[tile_ref[q]], preferred_element_type=jnp.float32)
+            gain = jnp.where(q < count, taper_ref[kind_ref[q]] * cross, 0.0)
+            gain_ref[q] = gain.astype(jnp.bfloat16)
+
+    w_copy.wait()
+
+    @pl.loop(0, steps)
+    def _(step):
         for u in range(UNROLL):
             q = step * UNROLL + u
-            t, k = tile_ref[q], kind_ref[q]
-            y = jnp.concatenate([held_ref[q, 0:128], held_ref[q, 128:256]], axis=1)
-            cross = jnp.dot(y, anom_ref[t], preferred_element_type=jnp.float32)
-            gain = jnp.where(q < count, taper_ref[k] * cross, 0.0).astype(jnp.bfloat16)
-            w = held_ref[q, members : 2 * members]
-            terms.append((t, jnp.dot(w, gain, preferred_element_type=jnp.float32)))
-        for t, term in terms:
-            acc_ref[t] += term
+            w = held_ref[obs_ref[q], members : 2 * members]
+            acc_ref[tile_ref[q]] += jnp.dot(w, gain_ref[q], preferred_element_type=jnp.float32)
 
-    @pl.loop(0, tiles, unroll=2)
+    @pl.loop(0, tiles, unroll=4)
     def _(t):
         out_ref[:, pl.ds(pl.multiple_of(t * width, width), width)] = acc_ref[t].astype(jnp.bfloat16)
 
@@ -98,8 +104,9 @@
         out_specs=vmem,
         scratch_shapes=[
             pltpu.VMEM((tiles, members, width), jnp.float32),
-            pltpu.VMEM((pairs, 2 * members, width), jnp.bfloat16),
-            pltpu.SemaphoreType.DMA((pairs,)),
+            pltpu.VMEM(blocks.shape, jnp.bfloat16),
+            pltpu.SemaphoreType.DMA((2,)),
+            pltpu.VMEM((pairs, width, width), jnp.bfloat16),
         ],
         compiler_params=pltpu.CompilerParams(vmem_limit_bytes=47 * 2**20),
         name="pairs",

time: 140 us -> 138 us (0.986)
  Pallas kernels: 6.53 us -> 4.47 us
    pallas_call x1, Pallas kernels: 5.47 us -> 3.41 us  [on_device(): pl.pallas_call(pair_kernel, out_shape=jax.ShapeDtypeStruct((members, cell...]
where the time goes in v4:
time: 138 us; the launch traced here: 136 us
  blocking collectives  65.2 us (47%)
  waiting for transfers between devices  32.6 us (24%)
  between operations  14.1 us (10%)
  local copies, waits for them, and re-layouts  8.66 us (6%)
  starting transfers between devices  7.93 us (6%)
  Pallas kernels  4.47 us (3%)
  other arithmetic  3.01 us (2%)
    all_to_all x1, blocking collectives, on_device(): sent = lax.all_to_all(sent, ('x', 'yl'), 0, 0, tiled=True)  31.7 us
    all_to_all x1, waiting for transfers between devices, on_device(): lax.all_to_all(jnp.broadcast_to(part, (X, Y * rows, cells)), 'x', 0, 0, t...  20.3 us
    all_to_all x1, blocking collectives, on_device(): lax.all_to_all(jnp.broadcast_to(ensemble[None], (Y, rows, cells)), y_axes...  19.7 us
    all_to_all x1, blocking collectives, on_device(): lax.all_to_all(summed.reshape(YH, rows, cells), 'yh', 0, 0, tiled=True)  13.9 us
    all_gather x1, waiting for transfers between devices, on_device(): blocks = lax.all_gather(blocks, ('z', 'core'), axis=0)  12.3 us
    all_to_all x1, starting transfers between devices, on_device(): lax.all_to_all(jnp.broadcast_to(part, (X, Y * rows, cells)), 'x', 0, 0, t...  7.93 us
    unnamed x15, local copies, waits for them, and re-layouts  4.32 us
    pallas_call x1, Pallas kernels, on_device(): pl.pallas_call(pair_kernel, out_shape=jax.ShapeDtypeStruct((members, cell...  3.41 us
  transfers between devices with their start and end apart: 2, of which 2 were waited for; matrix products, arithmetic and copies ran while one was open for 4% of the time, Pallas kernels for 1%

profile of v4, /device:TPU:1, one launch (start us, length us, event | category | flops | bytes accessed | tf_op | source)
XLA Modules:
  0.0 136.0 jit_solution(10823914607780426383)
XLA Ops:
  6.5 0.0 all-gather.3.cloned.1.call-start
  6.5 0.8 slice_bitcast_fusion.1
  7.3 0.1 copy.14
  7.4 0.1 copy.15
  7.6 0.9 copy.13
  8.4 0.7 pad_maximum_fusion
  9.1 0.0 all-gather.3.cloned.1.call-update
  9.1 0.9 broadcast_in_dim.6
  10.0 19.7 %all_to_all.20 = bf16[8,8,4096]{2,1,0:T(8,128)(2,1)S(1)} all-to-all(bf16[8,8,4096]{2,1,0:T(8,128)(2,1)S(1)} %broadcast_in_dim.6), channel_id=1, replica_groups=mesh['z'=12,'core'=2,'x'=4,'yh'=4,'yl'=2] {'yh','yl'}, dimensions={0} | all-to-all | bytes 1048576 | tf_op jit(solution)/shard_map/all_to_all | solution.py:84
  29.6 1.6 %broadcast_in_dim.15 = bf16[4,64,4096]{2,1,0:T(8,128)(2,1)} broadcast(bf16[64,4096]{1,0:T(8,128)(2,1)S(1)} %bitcast.26), dimensions={1,2} | broadcast | bytes 2621440 | tf_op jit(solution)/shard_map/broadcast_in_dim | solution.py:88
  31.2 0.0 copy-start.5
  31.2 7.9 %all-to-all-start.1 = ((bf16[4,64,4096]{2,1,0:T(8,128)(2,1)}), bf16[4,64,4096]{2,1,0:T(8,128)(2,1)S(1)}, u32[]{:S(2)}, u32[]{:S(2)}) async-start(bf16[4,64,4096]{2,1,0:T(8,128)(2,1)} %broadcast_in_dim.15), calls=%async_computation.1 | async-start | bytes 4194304 | tf_op jit(solution)/shard_map/all_to_all | solution.py:88
  39.2 0.0 copy-done.5
  39.2 1.3 copy.16
  41.2 1.3 multiply_bitcast_fusion.taper_ref
  42.5 20.3 %all-to-all-done.1 = bf16[4,64,4096]{2,1,0:T(8,128)(2,1)S(1)} async-done(((bf16[4,64,4096]{2,1,0:T(8,128)(2,1)}), bf16[4,64,4096]{2,1,0:T(8,128)(2,1)S(1)}, u32[]{:S(2)}, u32[]{:S(2)}) %all-to-all-start.1) | async-done | bytes 2097184 | tf_op jit(solution)/shard_map/all_to_all | solution.py:88
  62.8 0.0 copy-start
  62.8 1.3 copy-done
  64.1 0.0 copy-start.1
  64.1 1.6 %copy-done.1 = bf16[4,64,4096]{2,1,0:T(8,128)(2,1)S(1)} copy-done((bf16[4,64,4096]{2,1,0:T(8,128)(2,1)S(1)}, bf16[4,64,4096]{2,1,0:T(8,128)(2,1)}, u32[]{:S(2)}) %copy-start.1) | copy-done | bytes 2097176
  65.8 0.0 copy-start.2
  65.8 0.0 copy-start.3
  65.8 0.0 copy-start.4
  65.8 1.1 anomalies.1.anom_ref
  66.8 12.3 %all-gather.3.cloned.1.call-done = bf16[12288,128]{1,0:T(8,128)(2,1)} async-done(((bf16[512,128]{1,0:T(8,128)(2,1)}), bf16[12288,128]{1,0:T(8,128)(2,1)}) %all-gather.3.cloned.1.call-update) | async-done | bytes 3145744 | tf_op jit(solution)/shard_map/all_gather | solution.py:82
  79.1 0.0 copy-done.2
  79.1 0.0 copy-done.3
  79.1 0.0 copy-done.4
  79.1 3.4 %pairs.1 = bf16[256,4096]{1,0:T(8,128)(2,1)S(1)} custom-call(s32[32]{0:T(128)S(1)} %bitcast.22, s32[32]{0:T(128)S(1)} %bitcast.23, s32[32]{0:T(128)S(1)} %bitcast.24, s32[1]{0:T(128)} %bitcast.19.count_ref, bf16[32,256,128]{2,1,0:T(8,128)(2,1)S(1)} %anomalies.1.anom_ref, bf16[24,512,128]{2,1,0:T(8,128)(2,1)} %bitcast.25, ...), custom_call_target="tpu_custom_call" | custom-call | tf_op jit(solution)/shard_map/pairs/pallas_call | solution.py:100
  82.5 31.7 %all_to_all.21 = bf16[8,32,4096]{2,1,0:T(8,128)(2,1)S(1)} all-to-all(bf16[8,32,4096]{2,1,0:T(8,128)(2,1)S(1)} %bitcast.20), channel_id=1, replica_groups=mesh['z'=12,'core'=2,'x'=4,'yh'=4,'yl'=2] {'x','yl'}, dimensions={0} | all-to-all | bytes 4194304 | tf_op jit(solution)/shard_map/all_to_all | solution.py:115
  114.2 0.0 copy-start.6
  114.2 0.3 reduce_sum.21
  114.6 13.9 %all_to_all.22 = bf16[4,8,4096]{2,1,0:T(8,128)(2,1)S(1)} all-to-all(bf16[4,8,4096]{2,1,0:T(8,128)(2,1)S(1)} %bitcast.27), channel_id=1, replica_groups=mesh['z'=12,'core'=2,'x'=4,'yh'=4,'yl'=2] {'yh'}, dimensions={0} | all-to-all | bytes 524288 | tf_op jit(solution)/shard_map/all_to_all | solution.py:117
  128.5 0.0 copy-done.6
  128.5 0.7 add_convert_fusion
  (1 shorter events, 0.0 us)
Async XLA Ops:
  6.5 72.5 %all-gather.3.cloned.1.call-start = ((), (), s32[]{:S(2)}) async-start(), calls=%async_computation.4 | async-start | bytes 3276800 | tf_op jit(solution)/shard_map/all_gather | solution.py:82
  31.2 7.9 %copy-start.5 = (f32[16,128,128]{2,1,0:T(8,128)S(1)}, f32[16,128,128]{2,1,0:T(8,128)}, u32[]{:S(2)}) copy-start(f32[16,128,128]{2,1,0:T(8,128)} %param.11) | copy-start | bytes 3145732
  31.2 31.6 %all-to-all-start.1 = ((bf16[4,64,4096]{2,1,0:T(8,128)(2,1)}), bf16[4,64,4096]{2,1,0:T(8,128)(2,1)S(1)}, u32[]{:S(2)}, u32[]{:S(2)}) async-start(bf16[4,64,4096]{2,1,0:T(8,128)(2,1)} %broadcast_in_dim.15), calls=%async_computation.1 | async-start | bytes 4194304 | tf_op jit(solution)/shard_map/all_to_all | solution.py:88
  62.8 1.4 copy-start
  64.1 1.6 %copy-start.1 = (bf16[4,64,4096]{2,1,0:T(8,128)(2,1)S(1)}, bf16[4,64,4096]{2,1,0:T(8,128)(2,1)}, u32[]{:S(2)}) copy-start(bf16[4,64,4096]{2,1,0:T(8,128)(2,1)} %copy-done) | copy-start | bytes 6291460
  65.8 13.3 %copy-start.2 = (s32[1,1,32]{2,1,0:T(1,128)S(1)}, s32[1,1,32]{2,1,0:T(1,128)}, u32[]{:S(2)}) copy-start(s32[1,1,32]{2,1,0:T(1,128)} %param.13) | copy-start | bytes 388
  65.8 13.3 %copy-start.3 = (s32[1,1,32]{2,1,0:T(1,128)S(1)}, s32[1,1,32]{2,1,0:T(1,128)}, u32[]{:S(2)}) copy-start(s32[1,1,32]{2,1,0:T(1,128)} %param.12) | copy-start | bytes 388
  65.8 13.3 %copy-start.4 = (s32[1,1,32]{2,1,0:T(1,128)S(1)}, s32[1,1,32]{2,1,0:T(1,128)}, u32[]{:S(2)}) copy-start(s32[1,1,32]{2,1,0:T(1,128)} %param.14) | copy-start | bytes 388
  114.2 14.3 %copy-start.6 = (bf16[8,4096]{1,0:T(8,128)(2,1)S(1)}, bf16[8,4096]{1,0:T(8,128)(2,1)}, u32[]{:S(2)}) copy-start(bf16[8,4096]{1,0:T(8,128)(2,1)} %param.8) | copy-start | bytes 196612
Sparse Core Ops, SparseCore 0:
  9.8 69.2 all-gather.2

commit v5 on v4

--- a/solution.py
+++ b/solution.py
@@ -8,16 +8,6 @@
 Z, CORE, X, YH, YL = 12, 2, 4, 4, 2
 Y = YH * YL
 UNROLL = 16
-
-
-def anomaly_kernel(panel_ref, anom_ref):
-    tiles, members, width = anom_ref.shape
-
-    @pl.loop(0, tiles, unroll=2)
-    def _(t):
-        cells = panel_ref[:, pl.ds(pl.multiple_of(t * width, width), width)].astype(jnp.float32)
-        centre = jnp.sum(cells, axis=0, keepdims=True) * (1.0 / members)
-        anom_ref[t] = (cells - centre).astype(jnp.bfloat16)
 
 
 def pair_kernel(
@@ -48,7 +38,9 @@
         for u in range(UNROLL):
             q = step * UNROLL + u
             y = jnp.concatenate([held_ref[obs_ref[q], 0:128], held_ref[obs_ref[q], 128:256]], axis=1)
-            cross = jnp.dot(y, anom_ref[tile_ref[q]], preferred_element_type=jnp.float32)
+            start = pl.multiple_of(tile_ref[q] * width, width)
+            anom = anom_ref[:, pl.ds(start, width)]
+            cross = jnp.dot(y, anom, preferred_element_type=jnp.float32)
             gain = jnp.where(q < count, taper_ref[kind_ref[q]] * cross, 0.0)
             gain_ref[q] = gain.astype(jnp.bfloat16)
 
@@ -75,28 +67,26 @@
     tiles = cells // width
     pairs = pair_tile.shape[2]
     half = members // 2
-    weight = obs_weight.reshape(X, YH, YL, rows, width).transpose(0, 2, 1, 3, 4)
+
+    def reorder(array):
+        split = array.reshape(X, YH, YL, rows, width)
+        return split.transpose(0, 2, 1, 3, 4).reshape(members, width)
+
+    anomalies = reorder(obs_anom)
     blocks = jnp.concatenate(
-        [obs_anom[:half].T, obs_anom[half:].T, weight.reshape(members, width)], axis=0
+        [anomalies[:half].T, anomalies[half:].T, reorder(obs_weight)], axis=0
     )
     blocks = lax.all_gather(blocks, ("z", "core"), axis=0)
-    y_axes = ("yh", "yl")
-    part = lax.all_to_all(
-        jnp.broadcast_to(ensemble[None], (Y, rows, cells)), y_axes, 0, 0, tiled=True
-    )
-    part = part.reshape(1, Y * rows, cells)
-    panel = lax.all_to_all(jnp.broadcast_to(part, (X, Y * rows, cells)), "x", 0, 0, tiled=True)
+    part = jnp.broadcast_to(ensemble[None], (YH, rows, cells))
+    part = lax.all_to_all(part, "yh", 0, 0, tiled=True).reshape(1, YH * rows, cells)
+    panel = jnp.broadcast_to(part, (X * YL, YH * rows, cells))
+    panel = lax.all_to_all(panel, ("x", "yl"), 0, 0, tiled=True)
+    panel = panel.reshape(members, cells).astype(jnp.float32)
+    centre = jnp.sum(panel, axis=0, keepdims=True) * (1.0 / members)
+    anom = (panel - centre).astype(jnp.bfloat16)
     tapers = jnp.swapaxes(taper_table, 1, 2) * (1.0 / (members - 1))
     smem = pl.BlockSpec(memory_space=pltpu.SMEM)
     vmem = pl.BlockSpec(memory_space=pltpu.VMEM)
-    anom = pl.pallas_call(
-        anomaly_kernel,
-        out_shape=jax.ShapeDtypeStruct((tiles, members, width), jnp.bfloat16),
-        in_specs=[vmem],
-        out_specs=vmem,
-        compiler_params=pltpu.CompilerParams(vmem_limit_bytes=10 * 2**20),
-        name="anomalies",
-    )(panel.reshape(members, cells))
     partial = pl.pallas_call(
         pair_kernel,
         out_shape=jax.ShapeDtypeStruct((members, cells), jnp.bfloat16),

time: 138 us -> 138 us (level)
  waiting for transfers between devices: 32.6 us -> 39.7 us
  blocking collectives: 65.2 us -> 61.4 us
  starting transfers between devices: 7.93 us -> 4.44 us
  other arithmetic: 3.01 us -> 5.47 us
  local copies, waits for them, and re-layouts: 8.66 us -> 6.69 us
    all_gather x1, waiting for transfers between devices: 12.3 us -> 21.4 us  [on_device(): blocks = lax.all_gather(blocks, ('z', 'core'), axis=0)]
    all_to_all x1, starting transfers between devices: 7.93 us -> 4.44 us  [on_device(): panel = lax.all_to_all(panel, ('x', 'yl'), 0, 0, tiled=True)]
    all_to_all x1, blocking collectives: 19.7 us -> 16.4 us  [on_device(): lax.all_to_all(part, 'yh', 0, 0, tiled=True).reshape(1, YH * rows, cells)]
    convert_element_type x0 -> x1, other arithmetic: none -> 2.12 us  [on_device(): anom = (panel - centre).astype(jnp.bfloat16)]
    all_to_all x1, waiting for transfers between devices: 20.3 us -> 18.2 us  [on_device(): panel = lax.all_to_all(panel, ('x', 'yl'), 0, 0, tiled=True)]
    unnamed x15 -> x13, local copies, waits for them, and re-layouts: 4.32 us -> 2.36 us
    all_to_all x1, blocking collectives: 13.9 us -> 12.4 us  [on_device(): lax.all_to_all(summed.reshape(YH, rows, cells), 'yh', 0, 0, tiled=True)]
  transfers between devices with their start and end apart: 2 -> 2, of which waited for: 2 -> 2; matrix products, arithmetic and copies ran while one was open for 4% -> 6% of each run, Pallas kernels for 1% -> 0%
where the time goes in v5:
time: 138 us; the launch traced here: 136 us
  blocking collectives  61.4 us (44%)
  waiting for transfers between devices  39.7 us (29%)
  between operations  14.1 us (10%)
  local copies, waits for them, and re-layouts  6.69 us (5%)
  other arithmetic  5.47 us (4%)
  Pallas kernels  4.46 us (3%)
  starting transfers between devices  4.44 us (3%)
    all_to_all x1, blocking collectives, on_device(): sent = lax.all_to_all(sent, ('x', 'yl'), 0, 0, tiled=True)  32.6 us
    all_gather x1, waiting for transfers between devices, on_device(): blocks = lax.all_gather(blocks, ('z', 'core'), axis=0)  21.4 us
    all_to_all x1, waiting for transfers between devices, on_device(): panel = lax.all_to_all(panel, ('x', 'yl'), 0, 0, tiled=True)  18.2 us
    all_to_all x1, blocking collectives, on_device(): lax.all_to_all(part, 'yh', 0, 0, tiled=True).reshape(1, YH * rows, cells)  16.4 us
    all_to_all x1, blocking collectives, on_device(): lax.all_to_all(summed.reshape(YH, rows, cells), 'yh', 0, 0, tiled=True)  12.4 us
    pallas_call x1, Pallas kernels, on_device(): pl.pallas_call(pair_kernel, out_shape=jax.ShapeDtypeStruct((members, cell...  4.46 us
    all_to_all x1, starting transfers between devices, on_device(): panel = lax.all_to_all(panel, ('x', 'yl'), 0, 0, tiled=True)  4.44 us
  transfers between devices with their start and end apart: 2, of which 2 were waited for; matrix products, arithmetic and copies ran while one was open for 6% of the time, Pallas kernels for 0%

profile of v5, /device:TPU:1, one launch (start us, length us, event | category | flops | bytes accessed | tf_op | source)
XLA Modules:
  0.0 136.3 jit_solution(9867139701528121762)
XLA Ops:
  6.5 0.0 all-gather.3.cloned.1.call-start
  6.5 0.8 fusion.1
  7.3 0.1 copy.26
  7.5 0.1 copy.27
  7.6 0.9 copy.25
  8.4 0.7 pad_maximum_fusion
  9.1 0.0 all-gather.3.cloned.1.call-update
  9.1 0.9 broadcast_in_dim.6
  10.0 16.4 %all_to_all.20 = bf16[4,8,4096]{2,1,0:T(8,128)(2,1)S(1)} all-to-all(bf16[4,8,4096]{2,1,0:T(8,128)(2,1)S(1)} %broadcast_in_dim.6), channel_id=1, replica_groups=mesh['z'=12,'core'=2,'x'=4,'yh'=4,'yl'=2] {'yh'}, dimensions={0} | all-to-all | bytes 524288 | tf_op jit(solution)/shard_map/all_to_all | solution.py:81
  26.4 1.6 %broadcast_in_dim.16 = bf16[8,32,4096]{2,1,0:T(8,128)(2,1)} broadcast(bf16[32,4096]{1,0:T(8,128)(2,1)S(1)} %bitcast.34), dimensions={1,2} | broadcast | bytes 2359296 | tf_op jit(solution)/shard_map/broadcast_in_dim | solution.py:82
  28.0 0.0 copy-start.4
  28.0 4.4 %all-to-all-start.1 = ((bf16[8,32,4096]{2,1,0:T(8,128)(2,1)}), bf16[8,32,4096]{2,1,0:T(8,128)(2,1)S(1)}, u32[]{:S(2)}, u32[]{:S(2)}) async-start(bf16[8,32,4096]{2,1,0:T(8,128)(2,1)} %broadcast_in_dim.16), calls=%async_computation.1 | async-start | bytes 4194304 | tf_op jit(solution)/shard_map/all_to_all | solution.py:83
  32.5 0.0 copy-done.4
  32.5 1.3 copy.28
  34.5 1.3 multiply_bitcast_fusion.taper_ref
  35.8 18.2 %all-to-all-done.1 = bf16[8,32,4096]{2,1,0:T(8,128)(2,1)S(1)} async-done(((bf16[8,32,4096]{2,1,0:T(8,128)(2,1)}), bf16[8,32,4096]{2,1,0:T(8,128)(2,1)S(1)}, u32[]{:S(2)}, u32[]{:S(2)}) %all-to-all-start.1) | async-done | bytes 2097184 | tf_op jit(solution)/shard_map/all_to_all | solution.py:83
  54.0 0.0 copy-start.3
  54.0 0.3 convert_reduce_fusion
  54.4 1.0 copy-done.3
  55.4 0.0 copy-start
  55.4 0.0 copy-start.1
  55.4 0.0 copy-start.2
  55.4 2.1 %fusion.anom_ref = bf16[256,4096]{1,0:T(8,128)(2,1)S(1)} fusion(f32[4096]{0:T(1024)S(1)} %broadcast_multiply_fusion, bf16[8,32,4096]{2,1,0:T(8,128)(2,1)} %copy-done.3), kind=kLoop, calls=%fused_computation.1 | loop fusion | flops 3145728 | bytes 4210688 | tf_op jit(solution)/shard_map/convert_element_type | solution.py:86
  57.5 21.4 %all-gather.3.cloned.1.call-done = bf16[12288,128]{1,0:T(8,128)(2,1)} async-done(((bf16[512,128]{1,0:T(8,128)(2,1)}), bf16[12288,128]{1,0:T(8,128)(2,1)}) %all-gather.3.cloned.1.call-update) | async-done | bytes 3145744 | tf_op jit(solution)/shard_map/all_gather | solution.py:79
  79.0 0.0 copy-done
  79.0 0.0 copy-done.1
  79.0 0.0 copy-done.2
  79.0 4.5 %pairs.1 = bf16[256,4096]{1,0:T(8,128)(2,1)S(1)} custom-call(s32[32]{0:T(128)S(1)} %bitcast.29, s32[32]{0:T(128)S(1)} %bitcast.30, s32[32]{0:T(128)S(1)} %bitcast.31, s32[1]{0:T(128)} %bitcast.27.count_ref, bf16[256,4096]{1,0:T(8,128)(2,1)S(1)} %fusion.anom_ref, bf16[24,512,128]{2,1,0:T(8,128)(2,1)} %bitcast.32, ...), custom_call_target="tpu_custom_call" | custom-call | tf_op jit(solution)/shard_map/pairs/pallas_call | solution.py:90
  83.4 32.6 %all_to_all.21 = bf16[8,32,4096]{2,1,0:T(8,128)(2,1)S(1)} all-to-all(bf16[8,32,4096]{2,1,0:T(8,128)(2,1)S(1)} %bitcast.28), channel_id=1, replica_groups=mesh['z'=12,'core'=2,'x'=4,'yh'=4,'yl'=2] {'x','yl'}, dimensions={0} | all-to-all | bytes 4194304 | tf_op jit(solution)/shard_map/all_to_all | solution.py:105
  116.0 0.0 copy-start.5
  116.0 0.3 reduce_sum.31
  116.4 12.4 %all_to_all.22 = bf16[4,8,4096]{2,1,0:T(8,128)(2,1)S(1)} all-to-all(bf16[4,8,4096]{2,1,0:T(8,128)(2,1)S(1)} %bitcast.33), channel_id=1, replica_groups=mesh['z'=12,'core'=2,'x'=4,'yh'=4,'yl'=2] {'yh'}, dimensions={0} | all-to-all | bytes 524288 | tf_op jit(solution)/shard_map/all_to_all | solution.py:107
  128.8 0.0 copy-done.5
  128.8 0.7 add_convert_fusion
  (4 shorter events, 0.1 us)
Async XLA Ops:
  6.5 72.4 %all-gather.3.cloned.1.call-start = ((), (), s32[]{:S(2)}) async-start(), calls=%async_computation.4 | async-start | bytes 3276800 | tf_op jit(solution)/shard_map/all_gather | solution.py:79
  28.0 4.4 %copy-start.4 = (f32[16,128,128]{2,1,0:T(8,128)S(1)}, f32[16,128,128]{2,1,0:T(8,128)}, u32[]{:S(2)}) copy-start(f32[16,128,128]{2,1,0:T(8,128)} %param.11) | copy-start | bytes 3145732
  28.0 26.0 %all-to-all-start.1 = ((bf16[8,32,4096]{2,1,0:T(8,128)(2,1)}), bf16[8,32,4096]{2,1,0:T(8,128)(2,1)S(1)}, u32[]{:S(2)}, u32[]{:S(2)}) async-start(bf16[8,32,4096]{2,1,0:T(8,128)(2,1)} %broadcast_in_dim.16), calls=%async_computation.1 | async-start | bytes 4194304 | tf_op jit(solution)/shard_map/all_to_all | solution.py:83
  54.0 1.4 copy-start.3
  55.4 23.6 %copy-start = (s32[1,1,32]{2,1,0:T(1,128)S(1)}, s32[1,1,32]{2,1,0:T(1,128)}, u32[]{:S(2)}) copy-start(s32[1,1,32]{2,1,0:T(1,128)} %param.13) | copy-start | bytes 388
  55.4 23.6 %copy-start.1 = (s32[1,1,32]{2,1,0:T(1,128)S(1)}, s32[1,1,32]{2,1,0:T(1,128)}, u32[]{:S(2)}) copy-start(s32[1,1,32]{2,1,0:T(1,128)} %param.12) | copy-start | bytes 388
  55.4 23.6 %copy-start.2 = (s32[1,1,32]{2,1,0:T(1,128)S(1)}, s32[1,1,32]{2,1,0:T(1,128)}, u32[]{:S(2)}) copy-start(s32[1,1,32]{2,1,0:T(1,128)} %param.14) | copy-start | bytes 388
  116.0 12.8 %copy-start.5 = (bf16[8,4096]{1,0:T(8,128)(2,1)S(1)}, bf16[8,4096]{1,0:T(8,128)(2,1)}, u32[]{:S(2)}) copy-start(bf16[8,4096]{1,0:T(8,128)(2,1)} %param.8) | copy-start | bytes 196612
Sparse Core Ops, SparseCore 0:
  9.8 69.1 all-gather.2

commit v6 on v5

--- a/solution.py
+++ b/solution.py
@@ -5,8 +5,31 @@
 from jax.experimental.pallas import tpu as pltpu
 from jax.sharding import Mesh, PartitionSpec as P
 
-Z, CORE, X, YH, YL = 12, 2, 4, 4, 2
-Y = YH * YL
+Z, CORE, XH, XL, YH, YL = 12, 2, 2, 2, 4, 2
+X, Y = XH * XL, YH * YL
+FAR = ("xh", "yh")
+PLANES = ("core", "xh", "xl", "yh", "yl")
+
+
+def neighbour_blocks():
+    groups = []
+    for core in range(CORE):
+        for bx in range(XH):
+            for by in range(YH):
+                xs = sorted(((2 * bx + core + a) % X for a in range(2)), key=lambda x: x % 2)
+                ys = sorted(((2 * by + core + b) % Y for b in range(2)), key=lambda y: y % 2)
+                groups.append([(core * X + x) * Y + y for x in xs for y in ys])
+    return groups
+
+
+def near_exchange(array):
+    return lax.all_to_all(
+        array, PLANES, 0, 0, axis_index_groups=neighbour_blocks(), tiled=True
+    )
+
+
+def far_exchange(array):
+    return lax.all_to_all(array, FAR, 0, 0, tiled=True)
 UNROLL = 16
 
 
@@ -69,18 +92,17 @@
     half = members // 2
 
     def reorder(array):
-        split = array.reshape(X, YH, YL, rows, width)
-        return split.transpose(0, 2, 1, 3, 4).reshape(members, width)
+        split = array.reshape(XH, XL, YH, YL, rows, width)
+        return split.transpose(1, 3, 0, 2, 4, 5).reshape(members, width)
 
     anomalies = reorder(obs_anom)
     blocks = jnp.concatenate(
         [anomalies[:half].T, anomalies[half:].T, reorder(obs_weight)], axis=0
     )
     blocks = lax.all_gather(blocks, ("z", "core"), axis=0)
-    part = jnp.broadcast_to(ensemble[None], (YH, rows, cells))
-    part = lax.all_to_all(part, "yh", 0, 0, tiled=True).reshape(1, YH * rows, cells)
-    panel = jnp.broadcast_to(part, (X * YL, YH * rows, cells))
-    panel = lax.all_to_all(panel, ("x", "yl"), 0, 0, tiled=True)
+    part = far_exchange(jnp.broadcast_to(ensemble[None], (XH * YH, rows, cells)))
+    part = part.reshape(1, XH * YH * rows, cells)
+    panel = near_exchange(jnp.broadcast_to(part, (XL * YL, XH * YH * rows, cells)))
     panel = panel.reshape(members, cells).astype(jnp.float32)
     centre = jnp.sum(panel, axis=0, keepdims=True) * (1.0 / members)
     anom = (panel - centre).astype(jnp.bfloat16)
@@ -101,19 +123,18 @@
         compiler_params=pltpu.CompilerParams(vmem_limit_bytes=47 * 2**20),
         name="pairs",
     )(pair_tile[0, 0], pair_obs[0, 0], pair_taper[0, 0], pair_count[0], anom, blocks, tapers)
-    sent = partial.reshape(X * YL, YH * rows, cells)
-    sent = lax.all_to_all(sent, ("x", "yl"), 0, 0, tiled=True)
+    sent = near_exchange(partial.reshape(XL * YL, XH * YH * rows, cells))
     summed = jnp.sum(sent.astype(jnp.float32), axis=0).astype(jnp.bfloat16)
-    sent = lax.all_to_all(summed.reshape(YH, rows, cells), "yh", 0, 0, tiled=True)
+    sent = far_exchange(summed.reshape(XH * YH, rows, cells))
     update = jnp.sum(sent.astype(jnp.float32), axis=0)
     return (ensemble.astype(jnp.float32) + update).astype(jnp.bfloat16)
 
 
 def solution(mesh):
     fine = Mesh(
-        mesh.devices.reshape(Z, CORE, X, YH, YL), ("z", "core", "x", "yh", "yl")
+        mesh.devices.reshape(Z, CORE, XH, XL, YH, YL), ("z", "core", "xh", "xl", "yh", "yl")
     )
-    group, route = ("z", "core"), ("x", "yh", "yl")
+    group, route = ("z", "core"), ("xh", "xl", "yh", "yl")
     placed = (
         P(route, group),
         P(None, group + route),

time: 138 us -> 135 us (0.978); the launches traced: 136 us -> 135 us
  waiting for transfers between devices: 39.7 us -> 30.8 us
  blocking collectives: 61.4 us -> 70.2 us
    all_to_all x3, blocking collectives: 61.4 us -> 70.2 us  [the longest x2 47.9 us: far_exchange(): return lax.all_to_all(array, FAR, 0, 0, tiled=True)]
    all_to_all x1, waiting for transfers between devices: 18.2 us -> 11.7 us  [near_exchange(): lax.all_to_all(array, PLANES, 0, 0, axis_index_groups=neighbour_blocks(),...]
    all_gather x1, waiting for transfers between devices: 21.4 us -> 19.1 us  [on_device(): blocks = lax.all_gather(blocks, ('z', 'core'), axis=0)]
where the time goes in v6:
time: 135 us
  blocking collectives  70.2 us (52%)
  waiting for transfers between devices  30.8 us (23%)
  between operations  14.1 us (10%)
  local copies, waits for them, and re-layouts  6.71 us (5%)
  other arithmetic  5.55 us (4%)
  starting transfers between devices  3.76 us (3%)
  Pallas kernels  3.49 us (3%)
    all_to_all x2, blocking collectives, far_exchange(): return lax.all_to_all(array, FAR, 0, 0, tiled=True)  47.9 us
    all_to_all x1, blocking collectives, near_exchange(): lax.all_to_all(array, PLANES, 0, 0, axis_index_groups=neighbour_blocks(),...  22.3 us
    all_gather x1, waiting for transfers between devices, on_device(): blocks = lax.all_gather(blocks, ('z', 'core'), axis=0)  19.1 us
    all_to_all x1, waiting for transfers between devices, near_exchange(): lax.all_to_all(array, PLANES, 0, 0, axis_index_groups=neighbour_blocks(),...  11.7 us
    all_to_all x1, starting transfers between devices, near_exchange(): lax.all_to_all(array, PLANES, 0, 0, axis_index_groups=neighbour_blocks(),...  3.75 us
    pallas_call x1, Pallas kernels, on_device(): pl.pallas_call(pair_kernel, out_shape=jax.ShapeDtypeStruct((members, cell...  3.49 us
  transfers between devices with their start and end apart: 2, of which 2 were waited for; matrix products, arithmetic and copies ran while one was open for 6% of the time, Pallas kernels for 0%

profile of v6, /device:TPU:1, one launch (start us, length us, event | category | flops | bytes accessed | tf_op | source)
XLA Modules:
  0.0 134.6 jit_solution(12245353429943966186)
XLA Ops:
  6.5 0.0 all-gather.3.cloned.1.call-start
  6.5 0.8 fusion.1
  7.3 0.1 copy.26
  7.5 0.1 copy.27
  7.6 0.9 copy.25
  8.4 0.7 pad_maximum_fusion
  9.1 0.0 all-gather.3.cloned.1.call-update
  9.1 0.9 broadcast_in_dim.6
  10.0 26.2 %all_to_all.20 = bf16[8,8,4096]{2,1,0:T(8,128)(2,1)S(1)} all-to-all(bf16[8,8,4096]{2,1,0:T(8,128)(2,1)S(1)} %broadcast_in_dim.6), channel_id=1, replica_groups=mesh['z'=12,'core'=2,'xh'=2,'xl'=2,'yh'=4,'yl'=2] {'xh','yh'}, dimensions={0} | all-to-all | bytes 1048576 | tf_op jit(solution)/shard_map/all_to_all | solution.py:32
  36.3 1.6 %broadcast_in_dim.16 = bf16[4,64,4096]{2,1,0:T(8,128)(2,1)} broadcast(bf16[64,4096]{1,0:T(8,128)(2,1)S(1)} %bitcast.33), dimensions={1,2} | broadcast | bytes 2621440 | tf_op jit(solution)/shard_map/broadcast_in_dim | solution.py:105
  37.9 0.0 copy-start.4
  37.9 3.8 %all-to-all-start.1 = ((bf16[4,64,4096]{2,1,0:T(8,128)(2,1)}), bf16[4,64,4096]{2,1,0:T(8,128)(2,1)S(1)}, u32[]{:S(2)}, u32[]{:S(2)}) async-start(bf16[4,64,4096]{2,1,0:T(8,128)(2,1)} %broadcast_in_dim.16), calls=%async_computation.1 | async-start | bytes 4194304 | tf_op jit(solution)/shard_map/all_to_all | solution.py:26
  41.6 0.0 copy-done.4
  41.6 1.3 copy.28
  43.6 1.3 multiply_bitcast_fusion.taper_ref
  45.0 11.7 %all-to-all-done.1 = bf16[4,64,4096]{2,1,0:T(8,128)(2,1)S(1)} async-done(((bf16[4,64,4096]{2,1,0:T(8,128)(2,1)}), bf16[4,64,4096]{2,1,0:T(8,128)(2,1)S(1)}, u32[]{:S(2)}, u32[]{:S(2)}) %all-to-all-start.1) | async-done | bytes 2097184 | tf_op jit(solution)/shard_map/all_to_all | solution.py:26
  56.7 0.0 copy-start.3
  56.7 0.3 convert_reduce_fusion
  57.0 1.0 copy-done.3
  58.0 0.0 copy-start
  58.0 0.0 copy-start.1
  58.0 0.0 copy-start.2
  58.1 2.1 %fusion.anom_ref = bf16[256,4096]{1,0:T(8,128)(2,1)S(1)} fusion(f32[4096]{0:T(1024)S(1)} %broadcast_multiply_fusion, bf16[4,64,4096]{2,1,0:T(8,128)(2,1)} %copy-done.3), kind=kLoop, calls=%fused_computation.1 | loop fusion | flops 3145728 | bytes 4210688 | tf_op jit(solution)/shard_map/convert_element_type | solution.py:108
  60.2 19.1 %all-gather.3.cloned.1.call-done = bf16[12288,128]{1,0:T(8,128)(2,1)} async-done(((bf16[512,128]{1,0:T(8,128)(2,1)}), bf16[12288,128]{1,0:T(8,128)(2,1)}) %all-gather.3.cloned.1.call-update) | async-done | bytes 3145744 | tf_op jit(solution)/shard_map/all_gather | solution.py:102
  79.2 0.0 copy-done
  79.2 0.0 copy-done.1
  79.3 0.0 copy-done.2
  79.3 3.5 %pairs.1 = bf16[256,4096]{1,0:T(8,128)(2,1)S(1)} custom-call(s32[32]{0:T(128)S(1)} %bitcast.29, s32[32]{0:T(128)S(1)} %bitcast.30, s32[32]{0:T(128)S(1)} %bitcast.31, s32[1]{0:T(128)} %bitcast.27.count_ref, bf16[256,4096]{1,0:T(8,128)(2,1)S(1)} %fusion.anom_ref, bf16[24,512,128]{2,1,0:T(8,128)(2,1)} %bitcast.32, ...), custom_call_target="tpu_custom_call" | custom-call | tf_op jit(solution)/shard_map/pairs/pallas_call | solution.py:112
  82.8 22.3 %all_to_all.21 = bf16[4,64,4096]{2,1,0:T(8,128)(2,1)S(1)} all-to-all(bf16[4,64,4096]{2,1,0:T(8,128)(2,1)S(1)} %bitcast.28), channel_id=1, replica_groups={{0,1,8,9},{2,3,10,11},{4,5,12,13},{6,7,14,15},{16,17,24,25},{18,19,26,2..., dimensions={0} | all-to-all | bytes 4194304 | tf_op jit(solution)/shard_map/all_to_all | solution.py:26
  105.1 0.0 copy-start.5
  105.1 0.4 reduce_sum.31
  105.5 21.6 %all_to_all.22 = bf16[8,8,4096]{2,1,0:T(8,128)(2,1)S(1)} all-to-all(bf16[8,8,4096]{2,1,0:T(8,128)(2,1)S(1)} %bitcast.34), channel_id=1, replica_groups=mesh['z'=12,'core'=2,'xh'=2,'xl'=2,'yh'=4,'yl'=2] {'xh','yh'}, dimensions={0} | all-to-all | bytes 1048576 | tf_op jit(solution)/shard_map/all_to_all | solution.py:32
  127.1 0.1 convert_reduce_fusion.1
  127.1 0.0 copy-done.5
  127.2 0.7 add_convert_fusion
  (3 shorter events, 0.0 us)
Async XLA Ops:
  6.5 72.7 %all-gather.3.cloned.1.call-start = ((), (), s32[]{:S(2)}) async-start(), calls=%async_computation.4 | async-start | bytes 3276800 | tf_op jit(solution)/shard_map/all_gather | solution.py:102
  37.9 3.8 %copy-start.4 = (f32[16,128,128]{2,1,0:T(8,128)S(1)}, f32[16,128,128]{2,1,0:T(8,128)}, u32[]{:S(2)}) copy-start(f32[16,128,128]{2,1,0:T(8,128)} %param.11) | copy-start | bytes 3145732
  37.9 18.8 %all-to-all-start.1 = ((bf16[4,64,4096]{2,1,0:T(8,128)(2,1)}), bf16[4,64,4096]{2,1,0:T(8,128)(2,1)S(1)}, u32[]{:S(2)}, u32[]{:S(2)}) async-start(bf16[4,64,4096]{2,1,0:T(8,128)(2,1)} %broadcast_in_dim.16), calls=%async_computation.1 | async-start | bytes 4194304 | tf_op jit(solution)/shard_map/all_to_all | solution.py:26
  56.7 1.4 %copy-start.3 = (bf16[4,64,4096]{2,1,0:T(8,128)(2,1)}, bf16[4,64,4096]{2,1,0:T(8,128)(2,1)S(1)}, u32[]{:S(2)}) copy-start(bf16[4,64,4096]{2,1,0:T(8,128)(2,1)S(1)} %all-to-all-done.1) | copy-start | bytes 6291460
  58.0 21.2 %copy-start = (s32[1,1,32]{2,1,0:T(1,128)S(1)}, s32[1,1,32]{2,1,0:T(1,128)}, u32[]{:S(2)}) copy-start(s32[1,1,32]{2,1,0:T(1,128)} %param.13) | copy-start | bytes 388
  58.0 21.2 %copy-start.1 = (s32[1,1,32]{2,1,0:T(1,128)S(1)}, s32[1,1,32]{2,1,0:T(1,128)}, u32[]{:S(2)}) copy-start(s32[1,1,32]{2,1,0:T(1,128)} %param.12) | copy-start | bytes 388
  58.0 21.2 %copy-start.2 = (s32[1,1,32]{2,1,0:T(1,128)S(1)}, s32[1,1,32]{2,1,0:T(1,128)}, u32[]{:S(2)}) copy-start(s32[1,1,32]{2,1,0:T(1,128)} %param.14) | copy-start | bytes 388
  105.1 22.1 %copy-start.5 = (bf16[8,4096]{1,0:T(8,128)(2,1)S(1)}, bf16[8,4096]{1,0:T(8,128)(2,1)}, u32[]{:S(2)}) copy-start(bf16[8,4096]{1,0:T(8,128)(2,1)} %param.8) | copy-start | bytes 196612
Sparse Core Ops, SparseCore 0:
  9.8 69.4 all-gather.2

commit v7 on v6

--- a/solution.py
+++ b/solution.py
@@ -22,6 +22,54 @@
     return groups
 
 
+HX, KX = (0, 1, 1, 0), (0, 0, 1, 1)
+HY, KY, LY = (0, 1, 1, 0, 0, 1, 1, 0), (0, 0, 1, 0, 1, 1, 0, 1), (0, 0, 0, 1, 0, 1, 1, 1)
+
+
+def place(core, u, v):
+    return (u + core) % X * Y + (v + core) % Y
+
+
+def route_groups(same, order):
+    groups = []
+    for core in range(CORE):
+        found = {}
+        for u in range(X):
+            for v in range(Y):
+                member = (order(u, v), core * X * Y + place(core, u, v))
+                found.setdefault(same(u, v), []).append(member)
+        groups += [[device for _, device in sorted(found[key])] for key in sorted(found)]
+    return groups
+
+
+def first_groups():
+    return route_groups(lambda u, v: (u // 2, v // 2), lambda u, v: (HX[u], HY[v]))
+
+
+def second_groups():
+    return route_groups(
+        lambda u, v: ((u + 1) % X // 2, (v + 1) % Y // 2), lambda u, v: (KX[u], KY[v])
+    )
+
+
+def third_groups():
+    return route_groups(lambda u, v: (u, HY[v], KY[v]), lambda u, v: LY[v])
+
+
+def row_order(core):
+    keys = []
+    for u in range(X):
+        for v in range(Y):
+            keys.append(((HX[u], HY[v], KX[u], KY[v], LY[v]), place(core, u, v)))
+    return [owner for _, owner in sorted(keys)]
+
+
+def summed_exchange(array, groups):
+    parts = array.reshape(len(groups[0]), array.shape[0] // len(groups[0]), array.shape[1])
+    parts = lax.all_to_all(parts, PLANES, 0, 0, axis_index_groups=groups, tiled=True)
+    return jnp.sum(parts.astype(jnp.float32), axis=0)
+
+
 def near_exchange(array):
     return lax.all_to_all(
         array, PLANES, 0, 0, axis_index_groups=neighbour_blocks(), tiled=True
@@ -34,7 +82,7 @@
 
 
 def pair_kernel(
-    tile_ref, obs_ref, kind_ref, count_ref, anom_ref, blocks_ref, taper_ref, out_ref,
+    tile_ref, obs_ref, kind_ref, count_ref, core_ref, anom_ref, blocks_ref, taper_ref, out_ref,
     acc_ref, held_ref, sems, gain_ref,
 ):
     tiles, members, width = acc_ref.shape
@@ -76,9 +124,18 @@
             w = held_ref[obs_ref[q], members : 2 * members]
             acc_ref[tile_ref[q]] += jnp.dot(w, gain_ref[q], preferred_element_type=jnp.float32)
 
-    @pl.loop(0, tiles, unroll=4)
-    def _(t):
-        out_ref[:, pl.ds(pl.multiple_of(t * width, width), width)] = acc_ref[t].astype(jnp.bfloat16)
+    rows = members // (X * Y)
+    for core in range(CORE):
+        order = row_order(core)
+
+        @pl.when(core_ref[0] == core)
+        def _():
+            @pl.loop(0, tiles, unroll=2)
+            def _(t):
+                total = acc_ref[t]
+                total = jnp.concatenate([total[rows * r : rows * (r + 1)] for r in order], axis=0)
+                cells = pl.ds(pl.multiple_of(t * width, width), width)
+                out_ref[:, cells] = total.astype(jnp.bfloat16)
 
 
 def on_device(
@@ -97,7 +154,7 @@
 
     anomalies = reorder(obs_anom)
     blocks = jnp.concatenate(
-        [anomalies[:half].T, anomalies[half:].T, reorder(obs_weight)], axis=0
+        [anomalies[:half].T, anomalies[half:].T, obs_weight], axis=0
     )
     blocks = lax.all_gather(blocks, ("z", "core"), axis=0)
     part = far_exchange(jnp.broadcast_to(ensemble[None], (XH * YH, rows, cells)))
@@ -112,7 +169,7 @@
     partial = pl.pallas_call(
         pair_kernel,
         out_shape=jax.ShapeDtypeStruct((members, cells), jnp.bfloat16),
-        in_specs=[smem] * 4 + [vmem, pl.BlockSpec(memory_space=pltpu.HBM), vmem],
+        in_specs=[smem] * 5 + [vmem, pl.BlockSpec(memory_space=pltpu.HBM), vmem],
         out_specs=vmem,
         scratch_shapes=[
             pltpu.VMEM((tiles, members, width), jnp.float32),
@@ -122,11 +179,13 @@
         ],
         compiler_params=pltpu.CompilerParams(vmem_limit_bytes=47 * 2**20),
         name="pairs",
-    )(pair_tile[0, 0], pair_obs[0, 0], pair_taper[0, 0], pair_count[0], anom, blocks, tapers)
-    sent = near_exchange(partial.reshape(XL * YL, XH * YH * rows, cells))
-    summed = jnp.sum(sent.astype(jnp.float32), axis=0).astype(jnp.bfloat16)
-    sent = far_exchange(summed.reshape(XH * YH, rows, cells))
-    update = jnp.sum(sent.astype(jnp.float32), axis=0)
+    )(
+        pair_tile[0, 0], pair_obs[0, 0], pair_taper[0, 0], pair_count[0],
+        lax.axis_index("core").reshape(1), anom, blocks, tapers,
+    )
+    summed = summed_exchange(partial, first_groups()).astype(jnp.bfloat16)
+    summed = summed_exchange(summed, second_groups()).astype(jnp.bfloat16)
+    update = summed_exchange(summed, third_groups())
     return (ensemble.astype(jnp.float32) + update).astype(jnp.bfloat16)
 
 

time: 135 us -> 134 us (level)
  the two profiles are of different devices: /device:TPU:1 before, /device:TPU:8 now
where the time goes in v7:
time: 134 us
  blocking collectives  69.8 us (52%)
  waiting for transfers between devices  27.7 us (21%)
  between operations  14.1 us (11%)
  other arithmetic  6.39 us (5%)
  local copies, waits for them, and re-layouts  5.89 us (4%)
  starting transfers between devices  5.36 us (4%)
  Pallas kernels  4.48 us (3%)
    all_to_all x3, blocking collectives, summed_exchange(): lax.all_to_all(parts, PLANES, 0, 0, axis_index_groups=groups, tiled=True)  43.3 us
    all_to_all x1, blocking collectives, far_exchange(): return lax.all_to_all(array, FAR, 0, 0, tiled=True)  26.5 us
    all_gather x1, waiting for transfers between devices, on_device(): blocks = lax.all_gather(blocks, ('z', 'core'), axis=0)  16.5 us
    all_to_all x1, waiting for transfers between devices, near_exchange(): lax.all_to_all(array, PLANES, 0, 0, axis_index_groups=neighbour_blocks(),...  11.1 us
    all_to_all x1, starting transfers between devices, near_exchange(): lax.all_to_all(array, PLANES, 0, 0, axis_index_groups=neighbour_blocks(),...  5.36 us
    pallas_call x1, Pallas kernels, on_device(): pl.pallas_call(pair_kernel, out_shape=jax.ShapeDtypeStruct((members, cell...  4.48 us
  transfers between devices with their start and end apart: 2, of which 2 were waited for; matrix products, arithmetic and copies ran while one was open for 6% of the time, Pallas kernels for 0%

profile of v7, /device:TPU:8, one launch (start us, length us, event | category | flops | bytes accessed | tf_op | source)
XLA Modules:
  0.0 133.7 jit_solution(6810021521270549877)
XLA Ops:
  6.5 0.0 all-gather.3.cloned.1.call-start
  6.5 0.8 fusion.1
  7.3 0.1 copy.21
  7.5 0.1 copy.22
  7.6 1.5 %pad_maximum_fusion = bf16[512,128]{1,0:T(8,128)(2,1)} fusion(bf16[256,128]{1,0:T(8,128)(2,1)} %param.10, bf16[128,128]{1,0:T(8,128)(2,1)S(1)} %copy.22, bf16[128,128]{1,0:T(8,128)(2,1)S(1)} %copy.21), kind=kLoop, calls=%fused_computation.5 | loop fusion | flops 393216 | bytes 262144 | tf_op jit(solution)/shard_map/concatenate | solution.py:156
  9.1 0.0 all-gather.3.cloned.1.call-update
  9.1 0.9 broadcast_in_dim.6
  10.0 26.5 %all_to_all.25 = bf16[8,8,4096]{2,1,0:T(8,128)(2,1)S(1)} all-to-all(bf16[8,8,4096]{2,1,0:T(8,128)(2,1)S(1)} %broadcast_in_dim.6), channel_id=1, replica_groups=mesh['z'=12,'core'=2,'xh'=2,'xl'=2,'yh'=4,'yl'=2] {'xh','yh'}, dimensions={0} | all-to-all | bytes 1048576 | tf_op jit(solution)/shard_map/all_to_all | solution.py:80
  36.5 1.6 %broadcast_in_dim.16 = bf16[4,64,4096]{2,1,0:T(8,128)(2,1)} broadcast(bf16[64,4096]{1,0:T(8,128)(2,1)S(1)} %bitcast.31), dimensions={1,2} | broadcast | bytes 2621440 | tf_op jit(solution)/shard_map/broadcast_in_dim | solution.py:162
  38.1 0.0 copy-start.4
  38.1 5.4 %all-to-all-start.1 = ((bf16[4,64,4096]{2,1,0:T(8,128)(2,1)}), bf16[4,64,4096]{2,1,0:T(8,128)(2,1)S(1)}, u32[]{:S(2)}, u32[]{:S(2)}) async-start(bf16[4,64,4096]{2,1,0:T(8,128)(2,1)} %broadcast_in_dim.16), calls=%async_computation.1 | async-start | bytes 4194304 | tf_op jit(solution)/shard_map/all_to_all | solution.py:74
  43.4 0.0 copy-done.4
  43.4 1.3 %copy.23 = f32[16,128,128]{1,2,0:T(8,128)} copy(f32[16,128,128]{2,1,0:T(8,128)S(1)} %copy-done.4) | data formatting | bytes 2097152 | tf_op args[3]
  45.4 1.3 multiply_bitcast_fusion.taper_ref
  46.8 11.1 %all-to-all-done.1 = bf16[4,64,4096]{2,1,0:T(8,128)(2,1)S(1)} async-done(((bf16[4,64,4096]{2,1,0:T(8,128)(2,1)}), bf16[4,64,4096]{2,1,0:T(8,128)(2,1)S(1)}, u32[]{:S(2)}, u32[]{:S(2)}) %all-to-all-start.1) | async-done | bytes 2097184 | tf_op jit(solution)/shard_map/all_to_all | solution.py:74
  57.9 0.0 copy-start.3
  57.9 0.3 convert_reduce_fusion
  58.2 1.0 copy-done.3
  59.3 0.0 copy-start
  59.3 0.0 copy-start.1
  59.3 0.0 copy-start.2
  59.3 2.1 %fusion.anom_ref = bf16[256,4096]{1,0:T(8,128)(2,1)S(1)} fusion(f32[4096]{0:T(1024)S(1)} %broadcast_multiply_fusion, bf16[4,64,4096]{2,1,0:T(8,128)(2,1)} %copy-done.3), kind=kLoop, calls=%fused_computation.1 | loop fusion | flops 3145728 | bytes 4210688 | tf_op jit(solution)/shard_map/convert_element_type | solution.py:165
  61.4 16.5 %all-gather.3.cloned.1.call-done = bf16[12288,128]{1,0:T(8,128)(2,1)} async-done(((bf16[512,128]{1,0:T(8,128)(2,1)}), bf16[12288,128]{1,0:T(8,128)(2,1)}) %all-gather.3.cloned.1.call-update) | async-done | bytes 3145744 | tf_op jit(solution)/shard_map/all_gather | solution.py:159
  77.9 0.0 copy-done
  77.9 0.0 copy-done.1
  77.9 0.0 copy-done.2
  77.9 4.5 %pairs.1 = bf16[256,4096]{1,0:T(8,128)(2,1)S(1)} custom-call(s32[32]{0:T(128)S(1)} %bitcast.27, s32[32]{0:T(128)S(1)} %bitcast.28, s32[32]{0:T(128)S(1)} %bitcast.29, s32[1]{0:T(128)} %bitcast.25.count_ref, s32[1]{0:T(128)} %bitcast.4.core_ref, bf16[256,4096]{1,0:T(8,128)(2,1)S(1)} %fusion.anom_ref, bf16[24,512,128]{2,1,0:T(8,128)(2,1)} %bitcast.30, ...), custom_call_target="tpu_custom_call" | custom-call | tf_op jit(solution)/shard_map/pairs/pallas_call | solution.py:169
  82.4 17.5 %all_to_all.26 = bf16[4,64,4096]{2,1,0:T(8,128)(2,1)S(1)} all-to-all(bf16[4,64,4096]{2,1,0:T(8,128)(2,1)S(1)} %bitcast.26), channel_id=1, replica_groups={{0,1,8,9},{3,2,11,10},{4,5,12,13},{7,6,15,14},{24,25,16,17},{27,26,19,1..., dimensions={0} | all-to-all | bytes 4194304 | tf_op jit(solution)/shard_map/all_to_all | solution.py:69
  99.9 0.0 copy-start.5
  100.0 0.4 reduce_sum.43
  100.3 13.6 %all_to_all.27 = bf16[4,16,4096]{2,1,0:T(8,128)(2,1)S(1)} all-to-all(bf16[4,16,4096]{2,1,0:T(8,128)(2,1)S(1)} %bitcast.32), channel_id=1, replica_groups={{0,7,24,31},{1,2,25,26},{3,4,27,28},{6,5,30,29},{8,15,16,23},{9,10,17,1..., dimensions={0} | all-to-all | bytes 1048576 | tf_op jit(solution)/shard_map/all_to_all | solution.py:69
  114.0 0.1 reduce_sum.44
  114.1 12.1 %all_to_all.28 = bf16[2,8,4096]{2,1,0:T(8,128)(2,1)S(1)} all-to-all(bf16[2,8,4096]{2,1,0:T(8,128)(2,1)S(1)} %bitcast.33), channel_id=1, replica_groups={{0,3},{4,7},{1,6},{2,5},{8,11},{12,15},{9,14},{10,13},{16,19},{20,23},{..., dimensions={0} | all-to-all | bytes 262144 | tf_op jit(solution)/shard_map/all_to_all | solution.py:69
  126.2 0.0 copy-done.5
  126.2 0.7 add_convert_fusion
  (4 shorter events, 0.0 us)
Async XLA Ops:
  6.5 71.4 %all-gather.3.cloned.1.call-start = ((), (), s32[]{:S(2)}) async-start(), calls=%async_computation.5 | async-start | bytes 3276800 | tf_op jit(solution)/shard_map/all_gather | solution.py:159
  38.1 5.4 %copy-start.4 = (f32[16,128,128]{2,1,0:T(8,128)S(1)}, f32[16,128,128]{2,1,0:T(8,128)}, u32[]{:S(2)}) copy-start(f32[16,128,128]{2,1,0:T(8,128)} %param.11) | copy-start | bytes 3145732
  38.1 19.8 %all-to-all-start.1 = ((bf16[4,64,4096]{2,1,0:T(8,128)(2,1)}), bf16[4,64,4096]{2,1,0:T(8,128)(2,1)S(1)}, u32[]{:S(2)}, u32[]{:S(2)}) async-start(bf16[4,64,4096]{2,1,0:T(8,128)(2,1)} %broadcast_in_dim.16), calls=%async_computation.1 | async-start | bytes 4194304 | tf_op jit(solution)/shard_map/all_to_all | solution.py:74
  57.9 1.4 %copy-start.3 = (bf16[4,64,4096]{2,1,0:T(8,128)(2,1)}, bf16[4,64,4096]{2,1,0:T(8,128)(2,1)S(1)}, u32[]{:S(2)}) copy-start(bf16[4,64,4096]{2,1,0:T(8,128)(2,1)S(1)} %all-to-all-done.1) | copy-start | bytes 6291460
  59.3 18.7 %copy-start = (s32[1,1,32]{2,1,0:T(1,128)S(1)}, s32[1,1,32]{2,1,0:T(1,128)}, u32[]{:S(2)}) copy-start(s32[1,1,32]{2,1,0:T(1,128)} %param.13) | copy-start | bytes 388
  59.3 18.7 %copy-start.1 = (s32[1,1,32]{2,1,0:T(1,128)S(1)}, s32[1,1,32]{2,1,0:T(1,128)}, u32[]{:S(2)}) copy-start(s32[1,1,32]{2,1,0:T(1,128)} %param.12) | copy-start | bytes 388
  59.3 18.7 %copy-start.2 = (s32[1,1,32]{2,1,0:T(1,128)S(1)}, s32[1,1,32]{2,1,0:T(1,128)}, u32[]{:S(2)}) copy-start(s32[1,1,32]{2,1,0:T(1,128)} %param.14) | copy-start | bytes 388
  99.9 26.3 %copy-start.5 = (bf16[8,4096]{1,0:T(8,128)(2,1)S(1)}, bf16[8,4096]{1,0:T(8,128)(2,1)}, u32[]{:S(2)}) copy-start(bf16[8,4096]{1,0:T(8,128)(2,1)} %param.8) | copy-start | bytes 196612
Sparse Core Ops, SparseCore 0:
  9.8 68.0 all-gather.2

commit v8 on v7

--- a/solution.py
+++ b/solution.py
@@ -47,13 +47,7 @@
 
 
 def second_groups():
-    return route_groups(
-        lambda u, v: ((u + 1) % X // 2, (v + 1) % Y // 2), lambda u, v: (KX[u], KY[v])
-    )
-
-
-def third_groups():
-    return route_groups(lambda u, v: (u, HY[v], KY[v]), lambda u, v: LY[v])
+    return route_groups(lambda u, v: (HX[u], HY[v]), lambda u, v: (KX[u], KY[v], LY[v]))
 
 
 def row_order(core):
@@ -184,8 +178,7 @@
         lax.axis_index("core").reshape(1), anom, blocks, tapers,
     )
     summed = summed_exchange(partial, first_groups()).astype(jnp.bfloat16)
-    summed = summed_exchange(summed, second_groups()).astype(jnp.bfloat16)
-    update = summed_exchange(summed, third_groups())
+    update = summed_exchange(summed, second_groups())
     return (ensemble.astype(jnp.float32) + update).astype(jnp.bfloat16)
 
 

time: 134 us -> 135 us (level)
  the two profiles are of different devices: /device:TPU:8 before, /device:TPU:1 now
where the time goes in v8:
time: 135 us; the launch traced here: 134 us
  blocking collectives  68.9 us (51%)
  waiting for transfers between devices  30.8 us (23%)
  between operations  14.1 us (10%)
  other arithmetic  6.4 us (5%)
  local copies, waits for them, and re-layouts  5.84 us (4%)
  Pallas kernels  4.51 us (3%)
  starting transfers between devices  3.76 us (3%)
    all_to_all x2, blocking collectives, summed_exchange(): lax.all_to_all(parts, PLANES, 0, 0, axis_index_groups=groups, tiled=True)  42.6 us
    all_to_all x1, blocking collectives, far_exchange(): return lax.all_to_all(array, FAR, 0, 0, tiled=True)  26.2 us
    all_gather x1, waiting for transfers between devices, on_device(): blocks = lax.all_gather(blocks, ('z', 'core'), axis=0)  19.1 us
    all_to_all x1, waiting for transfers between devices, near_exchange(): lax.all_to_all(array, PLANES, 0, 0, axis_index_groups=neighbour_blocks(),...  11.7 us
    pallas_call x1, Pallas kernels, on_device(): pl.pallas_call(pair_kernel, out_shape=jax.ShapeDtypeStruct((members, cell...  4.51 us
    all_to_all x1, starting transfers between devices, near_exchange(): lax.all_to_all(array, PLANES, 0, 0, axis_index_groups=neighbour_blocks(),...  3.76 us
  transfers between devices with their start and end apart: 2, of which 2 were waited for; matrix products, arithmetic and copies ran while one was open for 6% of the time, Pallas kernels for 0%

profile of v8, /device:TPU:1, one launch (start us, length us, event | category | flops | bytes accessed | tf_op | source)
XLA Modules:
  0.0 134.4 jit_solution(17767996733127217310)
XLA Ops:
  6.5 0.0 all-gather.3.cloned.1.call-start
  6.5 0.8 fusion.1
  7.3 0.1 copy.21
  7.5 0.1 copy.22
  7.6 1.5 %pad_maximum_fusion = bf16[512,128]{1,0:T(8,128)(2,1)} fusion(bf16[256,128]{1,0:T(8,128)(2,1)} %param.10, bf16[128,128]{1,0:T(8,128)(2,1)S(1)} %copy.22, bf16[128,128]{1,0:T(8,128)(2,1)S(1)} %copy.21), kind=kLoop, calls=%fused_computation.5 | loop fusion | flops 393216 | bytes 262144 | tf_op jit(solution)/shard_map/concatenate | solution.py:150
  9.1 0.0 all-gather.3.cloned.1.call-update
  9.1 0.9 broadcast_in_dim.6
  10.0 26.2 %all_to_all.20 = bf16[8,8,4096]{2,1,0:T(8,128)(2,1)S(1)} all-to-all(bf16[8,8,4096]{2,1,0:T(8,128)(2,1)S(1)} %broadcast_in_dim.6), channel_id=1, replica_groups=mesh['z'=12,'core'=2,'xh'=2,'xl'=2,'yh'=4,'yl'=2] {'xh','yh'}, dimensions={0} | all-to-all | bytes 1048576 | tf_op jit(solution)/shard_map/all_to_all | solution.py:74
  36.2 1.6 %broadcast_in_dim.16 = bf16[4,64,4096]{2,1,0:T(8,128)(2,1)} broadcast(bf16[64,4096]{1,0:T(8,128)(2,1)S(1)} %bitcast.30), dimensions={1,2} | broadcast | bytes 2621440 | tf_op jit(solution)/shard_map/broadcast_in_dim | solution.py:156
  37.8 0.0 copy-start.4
  37.8 3.8 %all-to-all-start.1 = ((bf16[4,64,4096]{2,1,0:T(8,128)(2,1)}), bf16[4,64,4096]{2,1,0:T(8,128)(2,1)S(1)}, u32[]{:S(2)}, u32[]{:S(2)}) async-start(bf16[4,64,4096]{2,1,0:T(8,128)(2,1)} %broadcast_in_dim.16), calls=%async_computation.1 | async-start | bytes 4194304 | tf_op jit(solution)/shard_map/all_to_all | solution.py:68
  41.6 0.0 copy-done.4
  41.6 1.3 copy.23
  43.6 1.3 multiply_bitcast_fusion.taper_ref
  44.9 11.7 %all-to-all-done.1 = bf16[4,64,4096]{2,1,0:T(8,128)(2,1)S(1)} async-done(((bf16[4,64,4096]{2,1,0:T(8,128)(2,1)}), bf16[4,64,4096]{2,1,0:T(8,128)(2,1)S(1)}, u32[]{:S(2)}, u32[]{:S(2)}) %all-to-all-start.1) | async-done | bytes 2097184 | tf_op jit(solution)/shard_map/all_to_all | solution.py:68
  56.7 0.0 copy-start.3
  56.7 0.3 convert_reduce_fusion
  57.0 1.0 copy-done.3
  58.0 0.0 copy-start
  58.0 0.0 copy-start.1
  58.0 0.0 copy-start.2
  58.0 2.1 %fusion.anom_ref = bf16[256,4096]{1,0:T(8,128)(2,1)S(1)} fusion(f32[4096]{0:T(1024)S(1)} %broadcast_multiply_fusion, bf16[4,64,4096]{2,1,0:T(8,128)(2,1)} %copy-done.3), kind=kLoop, calls=%fused_computation.1 | loop fusion | flops 3145728 | bytes 4210688 | tf_op jit(solution)/shard_map/convert_element_type | solution.py:159
  60.2 19.1 %all-gather.3.cloned.1.call-done = bf16[12288,128]{1,0:T(8,128)(2,1)} async-done(((bf16[512,128]{1,0:T(8,128)(2,1)}), bf16[12288,128]{1,0:T(8,128)(2,1)}) %all-gather.3.cloned.1.call-update) | async-done | bytes 3145744 | tf_op jit(solution)/shard_map/all_gather | solution.py:153
  79.3 0.0 copy-done
  79.3 0.0 copy-done.1
  79.3 0.0 copy-done.2
  79.3 4.5 %pairs.1 = bf16[256,4096]{1,0:T(8,128)(2,1)S(1)} custom-call(s32[32]{0:T(128)S(1)} %bitcast.26, s32[32]{0:T(128)S(1)} %bitcast.27, s32[32]{0:T(128)S(1)} %bitcast.28, s32[1]{0:T(128)} %bitcast.24.count_ref, s32[1]{0:T(128)} %bitcast.4.core_ref, bf16[256,4096]{1,0:T(8,128)(2,1)S(1)} %fusion.anom_ref, bf16[24,512,128]{2,1,0:T(8,128)(2,1)} %bitcast.29, ...), custom_call_target="tpu_custom_call" | custom-call | tf_op jit(solution)/shard_map/pairs/pallas_call | solution.py:163
  83.8 22.3 %all_to_all.21 = bf16[4,64,4096]{2,1,0:T(8,128)(2,1)S(1)} all-to-all(bf16[4,64,4096]{2,1,0:T(8,128)(2,1)S(1)} %bitcast.25), channel_id=1, replica_groups={{0,1,8,9},{3,2,11,10},{4,5,12,13},{7,6,15,14},{24,25,16,17},{27,26,19,1..., dimensions={0} | all-to-all | bytes 4194304 | tf_op jit(solution)/shard_map/all_to_all | solution.py:63
  106.1 0.0 copy-start.5
  106.1 0.4 reduce_sum.31
  106.5 20.3 %all_to_all.22 = bf16[8,8,4096]{2,1,0:T(8,128)(2,1)S(1)} all-to-all(bf16[8,8,4096]{2,1,0:T(8,128)(2,1)S(1)} %bitcast.31), channel_id=1, replica_groups={{0,3,4,7,24,27,28,31},{1,6,2,5,25,30,26,29},{8,11,12,15,16,19,20,23},{9..., dimensions={0} | all-to-all | bytes 1048576 | tf_op jit(solution)/shard_map/all_to_all | solution.py:63
  126.8 0.1 convert_reduce_fusion.1
  126.9 0.0 copy-done.5
  126.9 0.7 add_convert_fusion
  (3 shorter events, 0.0 us)
Async XLA Ops:
  6.5 72.7 %all-gather.3.cloned.1.call-start = ((), (), s32[]{:S(2)}) async-start(), calls=%async_computation.4 | async-start | bytes 3276800 | tf_op jit(solution)/shard_map/all_gather | solution.py:153
  37.8 3.8 %copy-start.4 = (f32[16,128,128]{2,1,0:T(8,128)S(1)}, f32[16,128,128]{2,1,0:T(8,128)}, u32[]{:S(2)}) copy-start(f32[16,128,128]{2,1,0:T(8,128)} %param.11) | copy-start | bytes 3145732
  37.8 18.8 %all-to-all-start.1 = ((bf16[4,64,4096]{2,1,0:T(8,128)(2,1)}), bf16[4,64,4096]{2,1,0:T(8,128)(2,1)S(1)}, u32[]{:S(2)}, u32[]{:S(2)}) async-start(bf16[4,64,4096]{2,1,0:T(8,128)(2,1)} %broadcast_in_dim.16), calls=%async_computation.1 | async-start | bytes 4194304 | tf_op jit(solution)/shard_map/all_to_all | solution.py:68
  56.7 1.4 %copy-start.3 = (bf16[4,64,4096]{2,1,0:T(8,128)(2,1)}, bf16[4,64,4096]{2,1,0:T(8,128)(2,1)S(1)}, u32[]{:S(2)}) copy-start(bf16[4,64,4096]{2,1,0:T(8,128)(2,1)S(1)} %all-to-all-done.1) | copy-start | bytes 6291460
  58.0 21.2 %copy-start = (s32[1,1,32]{2,1,0:T(1,128)S(1)}, s32[1,1,32]{2,1,0:T(1,128)}, u32[]{:S(2)}) copy-start(s32[1,1,32]{2,1,0:T(1,128)} %param.13) | copy-start | bytes 388
  58.0 21.2 %copy-start.1 = (s32[1,1,32]{2,1,0:T(1,128)S(1)}, s32[1,1,32]{2,1,0:T(1,128)}, u32[]{:S(2)}) copy-start(s32[1,1,32]{2,1,0:T(1,128)} %param.12) | copy-start | bytes 388
  58.0 21.2 %copy-start.2 = (s32[1,1,32]{2,1,0:T(1,128)S(1)}, s32[1,1,32]{2,1,0:T(1,128)}, u32[]{:S(2)}) copy-start(s32[1,1,32]{2,1,0:T(1,128)} %param.14) | copy-start | bytes 388
  106.1 20.8 %copy-start.5 = (bf16[8,4096]{1,0:T(8,128)(2,1)S(1)}, bf16[8,4096]{1,0:T(8,128)(2,1)}, u32[]{:S(2)}) copy-start(bf16[8,4096]{1,0:T(8,128)(2,1)} %param.8) | copy-start | bytes 196612
Sparse Core Ops, SparseCore 0:
  9.8 69.4 all-gather.2

commit v9 on v7

--- a/solution.py
+++ b/solution.py
@@ -27,7 +27,7 @@
 
 
 def place(core, u, v):
-    return (u + core) % X * Y + (v + core) % Y
+    return (u + 1 - core) % X * Y + (v + core) % Y
 
 
 def route_groups(same, order):

time: 134 us -> 134 us (level)
  the two profiles are of different devices: /device:TPU:8 before, /device:TPU:2 now
where the time goes in v9:
time: 134 us; the launch traced here: 133 us
  blocking collectives  69 us (51%)
  waiting for transfers between devices  27.6 us (21%)
  between operations  14.1 us (11%)
  other arithmetic  6.39 us (5%)
  local copies, waits for them, and re-layouts  5.89 us (4%)
  starting transfers between devices  5.05 us (4%)
  Pallas kernels  4.5 us (3%)
    all_to_all x3, blocking collectives, summed_exchange(): lax.all_to_all(parts, PLANES, 0, 0, axis_index_groups=groups, tiled=True)  42.1 us
    all_to_all x1, blocking collectives, far_exchange(): return lax.all_to_all(array, FAR, 0, 0, tiled=True)  26.9 us
    all_gather x1, waiting for transfers between devices, on_device(): blocks = lax.all_gather(blocks, ('z', 'core'), axis=0)  16.4 us
    all_to_all x1, waiting for transfers between devices, near_exchange(): lax.all_to_all(array, PLANES, 0, 0, axis_index_groups=neighbour_blocks(),...  11.2 us
    all_to_all x1, starting transfers between devices, near_exchange(): lax.all_to_all(array, PLANES, 0, 0, axis_index_groups=neighbour_blocks(),...  5.05 us
    pallas_call x1, Pallas kernels, on_device(): pl.pallas_call(pair_kernel, out_shape=jax.ShapeDtypeStruct((members, cell...  4.5 us
  transfers between devices with their start and end apart: 2, of which 2 were waited for; matrix products, arithmetic and copies ran while one was open for 6% of the time, Pallas kernels for 0%

profile of v9, /device:TPU:2, one launch (start us, length us, event | category | flops | bytes accessed | tf_op | source)
XLA Modules:
  0.0 132.6 jit_solution(11249778581928625176)
XLA Ops:
  6.5 0.0 all-gather.3.cloned.1.call-start
  6.5 0.8 fusion.1
  7.3 0.1 copy.21
  7.5 0.1 copy.22
  7.6 1.5 %pad_maximum_fusion = bf16[512,128]{1,0:T(8,128)(2,1)} fusion(bf16[256,128]{1,0:T(8,128)(2,1)} %param.10, bf16[128,128]{1,0:T(8,128)(2,1)S(1)} %copy.22, bf16[128,128]{1,0:T(8,128)(2,1)S(1)} %copy.21), kind=kLoop, calls=%fused_computation.5 | loop fusion | flops 393216 | bytes 262144 | tf_op jit(solution)/shard_map/concatenate | solution.py:156
  9.1 0.0 all-gather.3.cloned.1.call-update
  9.1 0.9 broadcast_in_dim.6
  10.0 26.9 %all_to_all.25 = bf16[8,8,4096]{2,1,0:T(8,128)(2,1)S(1)} all-to-all(bf16[8,8,4096]{2,1,0:T(8,128)(2,1)S(1)} %broadcast_in_dim.6), channel_id=1, replica_groups=mesh['z'=12,'core'=2,'xh'=2,'xl'=2,'yh'=4,'yl'=2] {'xh','yh'}, dimensions={0} | all-to-all | bytes 1048576 | tf_op jit(solution)/shard_map/all_to_all | solution.py:80
  36.9 1.6 %broadcast_in_dim.16 = bf16[4,64,4096]{2,1,0:T(8,128)(2,1)} broadcast(bf16[64,4096]{1,0:T(8,128)(2,1)S(1)} %bitcast.31), dimensions={1,2} | broadcast | bytes 2621440 | tf_op jit(solution)/shard_map/broadcast_in_dim | solution.py:162
  38.5 0.0 copy-start.4
  38.5 5.0 %all-to-all-start.1 = ((bf16[4,64,4096]{2,1,0:T(8,128)(2,1)}), bf16[4,64,4096]{2,1,0:T(8,128)(2,1)S(1)}, u32[]{:S(2)}, u32[]{:S(2)}) async-start(bf16[4,64,4096]{2,1,0:T(8,128)(2,1)} %broadcast_in_dim.16), calls=%async_computation.1 | async-start | bytes 4194304 | tf_op jit(solution)/shard_map/all_to_all | solution.py:74
  43.5 0.0 copy-done.4
  43.5 1.3 %copy.23 = f32[16,128,128]{1,2,0:T(8,128)} copy(f32[16,128,128]{2,1,0:T(8,128)S(1)} %copy-done.4) | data formatting | bytes 2097152 | tf_op args[3]
  45.5 1.3 multiply_bitcast_fusion.taper_ref
  46.9 11.2 %all-to-all-done.1 = bf16[4,64,4096]{2,1,0:T(8,128)(2,1)S(1)} async-done(((bf16[4,64,4096]{2,1,0:T(8,128)(2,1)}), bf16[4,64,4096]{2,1,0:T(8,128)(2,1)S(1)}, u32[]{:S(2)}, u32[]{:S(2)}) %all-to-all-start.1) | async-done | bytes 2097184 | tf_op jit(solution)/shard_map/all_to_all | solution.py:74
  58.0 0.0 copy-start.3
  58.0 0.3 convert_reduce_fusion
  58.4 1.0 copy-done.3
  59.4 0.0 copy-start
  59.4 0.0 copy-start.1
  59.4 0.0 copy-start.2
  59.4 2.1 %fusion.anom_ref = bf16[256,4096]{1,0:T(8,128)(2,1)S(1)} fusion(f32[4096]{0:T(1024)S(1)} %broadcast_multiply_fusion, bf16[4,64,4096]{2,1,0:T(8,128)(2,1)} %copy-done.3), kind=kLoop, calls=%fused_computation.1 | loop fusion | flops 3145728 | bytes 4210688 | tf_op jit(solution)/shard_map/convert_element_type | solution.py:165
  61.5 16.4 %all-gather.3.cloned.1.call-done = bf16[12288,128]{1,0:T(8,128)(2,1)} async-done(((bf16[512,128]{1,0:T(8,128)(2,1)}), bf16[12288,128]{1,0:T(8,128)(2,1)}) %all-gather.3.cloned.1.call-update) | async-done | bytes 3145744 | tf_op jit(solution)/shard_map/all_gather | solution.py:159
  77.9 0.0 copy-done
  78.0 0.0 copy-done.1
  78.0 0.0 copy-done.2
  78.0 4.5 %pairs.1 = bf16[256,4096]{1,0:T(8,128)(2,1)S(1)} custom-call(s32[32]{0:T(128)S(1)} %bitcast.27, s32[32]{0:T(128)S(1)} %bitcast.28, s32[32]{0:T(128)S(1)} %bitcast.29, s32[1]{0:T(128)} %bitcast.25.count_ref, s32[1]{0:T(128)} %bitcast.4.core_ref, bf16[256,4096]{1,0:T(8,128)(2,1)S(1)} %fusion.anom_ref, bf16[24,512,128]{2,1,0:T(8,128)(2,1)} %bitcast.30, ...), custom_call_target="tpu_custom_call" | custom-call | tf_op jit(solution)/shard_map/pairs/pallas_call | solution.py:169
  82.5 18.0 %all_to_all.26 = bf16[4,64,4096]{2,1,0:T(8,128)(2,1)S(1)} all-to-all(bf16[4,64,4096]{2,1,0:T(8,128)(2,1)S(1)} %bitcast.26), channel_id=1, replica_groups={{8,9,16,17},{11,10,19,18},{12,13,20,21},{15,14,23,22},{0,1,24,25},{3,2,..., dimensions={0} | all-to-all | bytes 4194304 | tf_op jit(solution)/shard_map/all_to_all | solution.py:69
  100.5 0.0 copy-start.5
  100.5 0.4 reduce_sum.43
  100.9 14.5 %all_to_all.27 = bf16[4,16,4096]{2,1,0:T(8,128)(2,1)S(1)} all-to-all(bf16[4,16,4096]{2,1,0:T(8,128)(2,1)S(1)} %bitcast.32), channel_id=1, replica_groups={{8,15,0,7},{9,10,1,2},{11,12,3,4},{14,13,6,5},{16,23,24,31},{17,18,25,2..., dimensions={0} | all-to-all | bytes 1048576 | tf_op jit(solution)/shard_map/all_to_all | solution.py:69
  115.4 0.1 reduce_sum.44
  115.5 9.6 %all_to_all.28 = bf16[2,8,4096]{2,1,0:T(8,128)(2,1)S(1)} all-to-all(bf16[2,8,4096]{2,1,0:T(8,128)(2,1)S(1)} %bitcast.33), channel_id=1, replica_groups={{8,11},{12,15},{9,14},{10,13},{16,19},{20,23},{17,22},{18,21},{24,27},{..., dimensions={0} | all-to-all | bytes 262144 | tf_op jit(solution)/shard_map/all_to_all | solution.py:69
  125.1 0.0 copy-done.5
  125.1 0.7 add_convert_fusion
  (4 shorter events, 0.0 us)
Async XLA Ops:
  6.5 71.4 %all-gather.3.cloned.1.call-start = ((), (), s32[]{:S(2)}) async-start(), calls=%async_computation.5 | async-start | bytes 3276800 | tf_op jit(solution)/shard_map/all_gather | solution.py:159
  38.5 5.1 %copy-start.4 = (f32[16,128,128]{2,1,0:T(8,128)S(1)}, f32[16,128,128]{2,1,0:T(8,128)}, u32[]{:S(2)}) copy-start(f32[16,128,128]{2,1,0:T(8,128)} %param.11) | copy-start | bytes 3145732
  38.5 19.5 %all-to-all-start.1 = ((bf16[4,64,4096]{2,1,0:T(8,128)(2,1)}), bf16[4,64,4096]{2,1,0:T(8,128)(2,1)S(1)}, u32[]{:S(2)}, u32[]{:S(2)}) async-start(bf16[4,64,4096]{2,1,0:T(8,128)(2,1)} %broadcast_in_dim.16), calls=%async_computation.1 | async-start | bytes 4194304 | tf_op jit(solution)/shard_map/all_to_all | solution.py:74
  58.0 1.4 %copy-start.3 = (bf16[4,64,4096]{2,1,0:T(8,128)(2,1)}, bf16[4,64,4096]{2,1,0:T(8,128)(2,1)S(1)}, u32[]{:S(2)}) copy-start(bf16[4,64,4096]{2,1,0:T(8,128)(2,1)S(1)} %all-to-all-done.1) | copy-start | bytes 6291460
  59.4 18.6 %copy-start = (s32[1,1,32]{2,1,0:T(1,128)S(1)}, s32[1,1,32]{2,1,0:T(1,128)}, u32[]{:S(2)}) copy-start(s32[1,1,32]{2,1,0:T(1,128)} %param.13) | copy-start | bytes 388
  59.4 18.6 %copy-start.1 = (s32[1,1,32]{2,1,0:T(1,128)S(1)}, s32[1,1,32]{2,1,0:T(1,128)}, u32[]{:S(2)}) copy-start(s32[1,1,32]{2,1,0:T(1,128)} %param.12) | copy-start | bytes 388
  59.4 18.6 %copy-start.2 = (s32[1,1,32]{2,1,0:T(1,128)S(1)}, s32[1,1,32]{2,1,0:T(1,128)}, u32[]{:S(2)}) copy-start(s32[1,1,32]{2,1,0:T(1,128)} %param.14) | copy-start | bytes 388
  100.5 24.6 %copy-start.5 = (bf16[8,4096]{1,0:T(8,128)(2,1)S(1)}, bf16[8,4096]{1,0:T(8,128)(2,1)}, u32[]{:S(2)}) copy-start(bf16[8,4096]{1,0:T(8,128)(2,1)} %param.8) | copy-start | bytes 196612
Sparse Core Ops, SparseCore 0:
  9.8 68.1 all-gather.2

commit v10 on v9

--- a/solution.py
+++ b/solution.py
@@ -27,7 +27,7 @@
 
 
 def place(core, u, v):
-    return (u + 1 - core) % X * Y + (v + core) % Y
+    return (u + core) % X * Y + (v + 1 - core) % Y
 
 
 def route_groups(same, order):

time: 134 us -> 135 us (level)
  the two profiles are of different devices: /device:TPU:2 before, /device:TPU:8 now
where the time goes in v10:
time: 135 us
  blocking collectives  71.7 us (53%)
  waiting for transfers between devices  27.7 us (21%)
  between operations  14.1 us (10%)
  other arithmetic  6.39 us (5%)
  local copies, waits for them, and re-layouts  5.89 us (4%)
  starting transfers between devices  5.36 us (4%)
  Pallas kernels  3.52 us (3%)
    all_to_all x3, blocking collectives, summed_exchange(): lax.all_to_all(parts, PLANES, 0, 0, axis_index_groups=groups, tiled=True)  45.2 us
    all_to_all x1, blocking collectives, far_exchange(): return lax.all_to_all(array, FAR, 0, 0, tiled=True)  26.5 us
    all_gather x1, waiting for transfers between devices, on_device(): blocks = lax.all_gather(blocks, ('z', 'core'), axis=0)  16.5 us
    all_to_all x1, waiting for transfers between devices, near_exchange(): lax.all_to_all(array, PLANES, 0, 0, axis_index_groups=neighbour_blocks(),...  11.1 us
    all_to_all x1, starting transfers between devices, near_exchange(): lax.all_to_all(array, PLANES, 0, 0, axis_index_groups=neighbour_blocks(),...  5.36 us
    pallas_call x1, Pallas kernels, on_device(): pl.pallas_call(pair_kernel, out_shape=jax.ShapeDtypeStruct((members, cell...  3.52 us
  transfers between devices with their start and end apart: 2, of which 2 were waited for; matrix products, arithmetic and copies ran while one was open for 6% of the time, Pallas kernels for 0%

profile of v10, /device:TPU:8, one launch (start us, length us, event | category | flops | bytes accessed | tf_op | source)
XLA Modules:
  0.0 134.7 jit_solution(13524158907707341577)
XLA Ops:
  6.5 0.0 all-gather.3.cloned.1.call-start
  6.5 0.8 fusion.1
  7.3 0.1 copy.21
  7.5 0.1 copy.22
  7.6 1.5 %pad_maximum_fusion = bf16[512,128]{1,0:T(8,128)(2,1)} fusion(bf16[256,128]{1,0:T(8,128)(2,1)} %param.10, bf16[128,128]{1,0:T(8,128)(2,1)S(1)} %copy.22, bf16[128,128]{1,0:T(8,128)(2,1)S(1)} %copy.21), kind=kLoop, calls=%fused_computation.5 | loop fusion | flops 393216 | bytes 262144 | tf_op jit(solution)/shard_map/concatenate | solution.py:156
  9.1 0.0 all-gather.3.cloned.1.call-update
  9.1 0.9 broadcast_in_dim.6
  10.0 26.5 %all_to_all.25 = bf16[8,8,4096]{2,1,0:T(8,128)(2,1)S(1)} all-to-all(bf16[8,8,4096]{2,1,0:T(8,128)(2,1)S(1)} %broadcast_in_dim.6), channel_id=1, replica_groups=mesh['z'=12,'core'=2,'xh'=2,'xl'=2,'yh'=4,'yl'=2] {'xh','yh'}, dimensions={0} | all-to-all | bytes 1048576 | tf_op jit(solution)/shard_map/all_to_all | solution.py:80
  36.5 1.6 %broadcast_in_dim.16 = bf16[4,64,4096]{2,1,0:T(8,128)(2,1)} broadcast(bf16[64,4096]{1,0:T(8,128)(2,1)S(1)} %bitcast.31), dimensions={1,2} | broadcast | bytes 2621440 | tf_op jit(solution)/shard_map/broadcast_in_dim | solution.py:162
  38.1 0.0 copy-start.4
  38.1 5.4 %all-to-all-start.1 = ((bf16[4,64,4096]{2,1,0:T(8,128)(2,1)}), bf16[4,64,4096]{2,1,0:T(8,128)(2,1)S(1)}, u32[]{:S(2)}, u32[]{:S(2)}) async-start(bf16[4,64,4096]{2,1,0:T(8,128)(2,1)} %broadcast_in_dim.16), calls=%async_computation.1 | async-start | bytes 4194304 | tf_op jit(solution)/shard_map/all_to_all | solution.py:74
  43.4 0.0 copy-done.4
  43.4 1.3 %copy.23 = f32[16,128,128]{1,2,0:T(8,128)} copy(f32[16,128,128]{2,1,0:T(8,128)S(1)} %copy-done.4) | data formatting | bytes 2097152 | tf_op args[3]
  45.4 1.3 multiply_bitcast_fusion.taper_ref
  46.8 11.1 %all-to-all-done.1 = bf16[4,64,4096]{2,1,0:T(8,128)(2,1)S(1)} async-done(((bf16[4,64,4096]{2,1,0:T(8,128)(2,1)}), bf16[4,64,4096]{2,1,0:T(8,128)(2,1)S(1)}, u32[]{:S(2)}, u32[]{:S(2)}) %all-to-all-start.1) | async-done | bytes 2097184 | tf_op jit(solution)/shard_map/all_to_all | solution.py:74
  57.9 0.0 copy-start.3
  57.9 0.3 convert_reduce_fusion
  58.2 1.0 copy-done.3
  59.3 0.0 copy-start
  59.3 0.0 copy-start.1
  59.3 0.0 copy-start.2
  59.3 2.1 %fusion.anom_ref = bf16[256,4096]{1,0:T(8,128)(2,1)S(1)} fusion(f32[4096]{0:T(1024)S(1)} %broadcast_multiply_fusion, bf16[4,64,4096]{2,1,0:T(8,128)(2,1)} %copy-done.3), kind=kLoop, calls=%fused_computation.1 | loop fusion | flops 3145728 | bytes 4210688 | tf_op jit(solution)/shard_map/convert_element_type | solution.py:165
  61.4 16.5 %all-gather.3.cloned.1.call-done = bf16[12288,128]{1,0:T(8,128)(2,1)} async-done(((bf16[512,128]{1,0:T(8,128)(2,1)}), bf16[12288,128]{1,0:T(8,128)(2,1)}) %all-gather.3.cloned.1.call-update) | async-done | bytes 3145744 | tf_op jit(solution)/shard_map/all_gather | solution.py:159
  77.9 0.0 copy-done
  77.9 0.0 copy-done.1
  77.9 0.0 copy-done.2
  77.9 3.5 %pairs.1 = bf16[256,4096]{1,0:T(8,128)(2,1)S(1)} custom-call(s32[32]{0:T(128)S(1)} %bitcast.27, s32[32]{0:T(128)S(1)} %bitcast.28, s32[32]{0:T(128)S(1)} %bitcast.29, s32[1]{0:T(128)} %bitcast.25.count_ref, s32[1]{0:T(128)} %bitcast.4.core_ref, bf16[256,4096]{1,0:T(8,128)(2,1)S(1)} %fusion.anom_ref, bf16[24,512,128]{2,1,0:T(8,128)(2,1)} %bitcast.30, ...), custom_call_target="tpu_custom_call" | custom-call | tf_op jit(solution)/shard_map/pairs/pallas_call | solution.py:169
  81.5 20.0 %all_to_all.26 = bf16[4,64,4096]{2,1,0:T(8,128)(2,1)S(1)} all-to-all(bf16[4,64,4096]{2,1,0:T(8,128)(2,1)S(1)} %bitcast.26), channel_id=1, replica_groups={{1,2,9,10},{4,3,12,11},{5,6,13,14},{0,7,8,15},{25,26,17,18},{28,27,20,1..., dimensions={0} | all-to-all | bytes 4194304 | tf_op jit(solution)/shard_map/all_to_all | solution.py:69
  101.4 0.0 copy-start.5
  101.4 0.4 reduce_sum.43
  101.8 12.8 %all_to_all.27 = bf16[4,16,4096]{2,1,0:T(8,128)(2,1)S(1)} all-to-all(bf16[4,16,4096]{2,1,0:T(8,128)(2,1)S(1)} %bitcast.32), channel_id=1, replica_groups={{1,0,25,24},{2,3,26,27},{4,5,28,29},{7,6,31,30},{9,8,17,16},{10,11,18,1..., dimensions={0} | all-to-all | bytes 1048576 | tf_op jit(solution)/shard_map/all_to_all | solution.py:69
  114.6 0.1 reduce_sum.44
  114.7 12.4 %all_to_all.28 = bf16[2,8,4096]{2,1,0:T(8,128)(2,1)S(1)} all-to-all(bf16[2,8,4096]{2,1,0:T(8,128)(2,1)S(1)} %bitcast.33), channel_id=1, replica_groups={{1,4},{5,0},{2,7},{3,6},{9,12},{13,8},{10,15},{11,14},{17,20},{21,16},{..., dimensions={0} | all-to-all | bytes 262144 | tf_op jit(solution)/shard_map/all_to_all | solution.py:69
  127.1 0.0 copy-done.5
  127.2 0.7 add_convert_fusion
  (4 shorter events, 0.0 us)
Async XLA Ops:
  6.5 71.4 %all-gather.3.cloned.1.call-start = ((), (), s32[]{:S(2)}) async-start(), calls=%async_computation.5 | async-start | bytes 3276800 | tf_op jit(solution)/shard_map/all_gather | solution.py:159
  38.1 5.4 %copy-start.4 = (f32[16,128,128]{2,1,0:T(8,128)S(1)}, f32[16,128,128]{2,1,0:T(8,128)}, u32[]{:S(2)}) copy-start(f32[16,128,128]{2,1,0:T(8,128)} %param.11) | copy-start | bytes 3145732
  38.1 19.8 %all-to-all-start.1 = ((bf16[4,64,4096]{2,1,0:T(8,128)(2,1)}), bf16[4,64,4096]{2,1,0:T(8,128)(2,1)S(1)}, u32[]{:S(2)}, u32[]{:S(2)}) async-start(bf16[4,64,4096]{2,1,0:T(8,128)(2,1)} %broadcast_in_dim.16), calls=%async_computation.1 | async-start | bytes 4194304 | tf_op jit(solution)/shard_map/all_to_all | solution.py:74
  57.9 1.4 %copy-start.3 = (bf16[4,64,4096]{2,1,0:T(8,128)(2,1)}, bf16[4,64,4096]{2,1,0:T(8,128)(2,1)S(1)}, u32[]{:S(2)}) copy-start(bf16[4,64,4096]{2,1,0:T(8,128)(2,1)S(1)} %all-to-all-done.1) | copy-start | bytes 6291460
  59.3 18.7 %copy-start = (s32[1,1,32]{2,1,0:T(1,128)S(1)}, s32[1,1,32]{2,1,0:T(1,128)}, u32[]{:S(2)}) copy-start(s32[1,1,32]{2,1,0:T(1,128)} %param.13) | copy-start | bytes 388
  59.3 18.7 %copy-start.1 = (s32[1,1,32]{2,1,0:T(1,128)S(1)}, s32[1,1,32]{2,1,0:T(1,128)}, u32[]{:S(2)}) copy-start(s32[1,1,32]{2,1,0:T(1,128)} %param.12) | copy-start | bytes 388
  59.3 18.7 %copy-start.2 = (s32[1,1,32]{2,1,0:T(1,128)S(1)}, s32[1,1,32]{2,1,0:T(1,128)}, u32[]{:S(2)}) copy-start(s32[1,1,32]{2,1,0:T(1,128)} %param.14) | copy-start | bytes 388
  101.4 25.7 %copy-start.5 = (bf16[8,4096]{1,0:T(8,128)(2,1)S(1)}, bf16[8,4096]{1,0:T(8,128)(2,1)}, u32[]{:S(2)}) copy-start(bf16[8,4096]{1,0:T(8,128)(2,1)} %param.8) | copy-start | bytes 196612
Sparse Core Ops, SparseCore 0:
  9.8 68.0 all-gather.2

commit v11 on v8

--- a/solution.py
+++ b/solution.py
@@ -27,7 +27,7 @@
 
 
 def place(core, u, v):
-    return (u + core) % X * Y + (v + core) % Y
+    return (u + 1 - core) % X * Y + (v + core) % Y
 
 
 def route_groups(same, order):

time: 135 us -> 135 us (level)
  no operation moved by 1% of the time
where the time goes in v11:
time: 135 us; the launch traced here: 133 us
  blocking collectives  68.7 us (51%)
  waiting for transfers between devices  30.8 us (23%)
  between operations  14.1 us (10%)
  other arithmetic  6.4 us (5%)
  local copies, waits for them, and re-layouts  5.84 us (4%)
  starting transfers between devices  3.76 us (3%)
  Pallas kernels  3.53 us (3%)
    all_to_all x2, blocking collectives, summed_exchange(): lax.all_to_all(parts, PLANES, 0, 0, axis_index_groups=groups, tiled=True)  42.5 us
    all_to_all x1, blocking collectives, far_exchange(): return lax.all_to_all(array, FAR, 0, 0, tiled=True)  26.2 us
    all_gather x1, waiting for transfers between devices, on_device(): blocks = lax.all_gather(blocks, ('z', 'core'), axis=0)  19.1 us
    all_to_all x1, waiting for transfers between devices, near_exchange(): lax.all_to_all(array, PLANES, 0, 0, axis_index_groups=neighbour_blocks(),...  11.7 us
    all_to_all x1, starting transfers between devices, near_exchange(): lax.all_to_all(array, PLANES, 0, 0, axis_index_groups=neighbour_blocks(),...  3.76 us
    pallas_call x1, Pallas kernels, on_device(): pl.pallas_call(pair_kernel, out_shape=jax.ShapeDtypeStruct((members, cell...  3.53 us
  transfers between devices with their start and end apart: 2, of which 2 were waited for; matrix products, arithmetic and copies ran while one was open for 6% of the time, Pallas kernels for 0%

profile of v11, /device:TPU:1, one launch (start us, length us, event | category | flops | bytes accessed | tf_op | source)
XLA Modules:
  0.0 133.3 jit_solution(16001542814066507918)
XLA Ops:
  6.5 0.0 all-gather.3.cloned.1.call-start
  6.5 0.8 fusion.1
  7.3 0.1 copy.21
  7.5 0.1 copy.22
  7.6 1.5 %pad_maximum_fusion = bf16[512,128]{1,0:T(8,128)(2,1)} fusion(bf16[256,128]{1,0:T(8,128)(2,1)} %param.10, bf16[128,128]{1,0:T(8,128)(2,1)S(1)} %copy.22, bf16[128,128]{1,0:T(8,128)(2,1)S(1)} %copy.21), kind=kLoop, calls=%fused_computation.5 | loop fusion | flops 393216 | bytes 262144 | tf_op jit(solution)/shard_map/concatenate | solution.py:150
  9.1 0.0 all-gather.3.cloned.1.call-update
  9.1 0.9 broadcast_in_dim.6
  10.0 26.2 %all_to_all.20 = bf16[8,8,4096]{2,1,0:T(8,128)(2,1)S(1)} all-to-all(bf16[8,8,4096]{2,1,0:T(8,128)(2,1)S(1)} %broadcast_in_dim.6), channel_id=1, replica_groups=mesh['z'=12,'core'=2,'xh'=2,'xl'=2,'yh'=4,'yl'=2] {'xh','yh'}, dimensions={0} | all-to-all | bytes 1048576 | tf_op jit(solution)/shard_map/all_to_all | solution.py:74
  36.2 1.6 %broadcast_in_dim.16 = bf16[4,64,4096]{2,1,0:T(8,128)(2,1)} broadcast(bf16[64,4096]{1,0:T(8,128)(2,1)S(1)} %bitcast.30), dimensions={1,2} | broadcast | bytes 2621440 | tf_op jit(solution)/shard_map/broadcast_in_dim | solution.py:156
  37.8 0.0 copy-start.4
  37.8 3.8 %all-to-all-start.1 = ((bf16[4,64,4096]{2,1,0:T(8,128)(2,1)}), bf16[4,64,4096]{2,1,0:T(8,128)(2,1)S(1)}, u32[]{:S(2)}, u32[]{:S(2)}) async-start(bf16[4,64,4096]{2,1,0:T(8,128)(2,1)} %broadcast_in_dim.16), calls=%async_computation.1 | async-start | bytes 4194304 | tf_op jit(solution)/shard_map/all_to_all | solution.py:68
  41.6 0.0 copy-done.4
  41.6 1.3 %copy.23 = f32[16,128,128]{1,2,0:T(8,128)} copy(f32[16,128,128]{2,1,0:T(8,128)S(1)} %copy-done.4) | data formatting | bytes 2097152 | tf_op args[3]
  43.6 1.3 %multiply_bitcast_fusion.taper_ref = f32[16,128,128]{2,1,0:T(8,128)S(1)} fusion(f32[16,128,128]{1,2,0:T(8,128)} %copy.23), kind=kLoop, calls=%fused_computation.4 | loop fusion | flops 262144 | bytes 2097152 | tf_op jit(solution)/shard_map/mul | solution.py:160
  44.9 11.7 %all-to-all-done.1 = bf16[4,64,4096]{2,1,0:T(8,128)(2,1)S(1)} async-done(((bf16[4,64,4096]{2,1,0:T(8,128)(2,1)}), bf16[4,64,4096]{2,1,0:T(8,128)(2,1)S(1)}, u32[]{:S(2)}, u32[]{:S(2)}) %all-to-all-start.1) | async-done | bytes 2097184 | tf_op jit(solution)/shard_map/all_to_all | solution.py:68
  56.7 0.0 copy-start.3
  56.7 0.3 convert_reduce_fusion
  57.0 1.0 copy-done.3
  58.0 0.0 copy-start
  58.0 0.0 copy-start.1
  58.0 0.0 copy-start.2
  58.0 2.1 %fusion.anom_ref = bf16[256,4096]{1,0:T(8,128)(2,1)S(1)} fusion(f32[4096]{0:T(1024)S(1)} %broadcast_multiply_fusion, bf16[4,64,4096]{2,1,0:T(8,128)(2,1)} %copy-done.3), kind=kLoop, calls=%fused_computation.1 | loop fusion | flops 3145728 | bytes 4210688 | tf_op jit(solution)/shard_map/convert_element_type | solution.py:159
  60.2 19.1 %all-gather.3.cloned.1.call-done = bf16[12288,128]{1,0:T(8,128)(2,1)} async-done(((bf16[512,128]{1,0:T(8,128)(2,1)}), bf16[12288,128]{1,0:T(8,128)(2,1)}) %all-gather.3.cloned.1.call-update) | async-done | bytes 3145744 | tf_op jit(solution)/shard_map/all_gather | solution.py:153
  79.3 0.0 copy-done
  79.3 0.0 copy-done.1
  79.3 0.0 copy-done.2
  79.3 3.5 %pairs.1 = bf16[256,4096]{1,0:T(8,128)(2,1)S(1)} custom-call(s32[32]{0:T(128)S(1)} %bitcast.26, s32[32]{0:T(128)S(1)} %bitcast.27, s32[32]{0:T(128)S(1)} %bitcast.28, s32[1]{0:T(128)} %bitcast.24.count_ref, s32[1]{0:T(128)} %bitcast.4.core_ref, bf16[256,4096]{1,0:T(8,128)(2,1)S(1)} %fusion.anom_ref, bf16[24,512,128]{2,1,0:T(8,128)(2,1)} %bitcast.29, ...), custom_call_target="tpu_custom_call" | custom-call | tf_op jit(solution)/shard_map/pairs/pallas_call | solution.py:163
  82.8 19.9 %all_to_all.21 = bf16[4,64,4096]{2,1,0:T(8,128)(2,1)S(1)} all-to-all(bf16[4,64,4096]{2,1,0:T(8,128)(2,1)S(1)} %bitcast.25), channel_id=1, replica_groups={{8,9,16,17},{11,10,19,18},{12,13,20,21},{15,14,23,22},{0,1,24,25},{3,2,..., dimensions={0} | all-to-all | bytes 4194304 | tf_op jit(solution)/shard_map/all_to_all | solution.py:63
  102.7 0.0 copy-start.5
  102.7 0.4 reduce_sum.31
  103.1 22.6 %all_to_all.22 = bf16[8,8,4096]{2,1,0:T(8,128)(2,1)S(1)} all-to-all(bf16[8,8,4096]{2,1,0:T(8,128)(2,1)S(1)} %bitcast.31), channel_id=1, replica_groups={{8,11,12,15,0,3,4,7},{9,14,10,13,1,6,2,5},{16,19,20,23,24,27,28,31},{17..., dimensions={0} | all-to-all | bytes 1048576 | tf_op jit(solution)/shard_map/all_to_all | solution.py:63
  125.7 0.1 convert_reduce_fusion.1
  125.8 0.0 copy-done.5
  125.8 0.7 add_convert_fusion
  (3 shorter events, 0.0 us)
Async XLA Ops:
  6.5 72.7 %all-gather.3.cloned.1.call-start = ((), (), s32[]{:S(2)}) async-start(), calls=%async_computation.4 | async-start | bytes 3276800 | tf_op jit(solution)/shard_map/all_gather | solution.py:153
  37.8 3.8 %copy-start.4 = (f32[16,128,128]{2,1,0:T(8,128)S(1)}, f32[16,128,128]{2,1,0:T(8,128)}, u32[]{:S(2)}) copy-start(f32[16,128,128]{2,1,0:T(8,128)} %param.11) | copy-start | bytes 3145732
  37.8 18.8 %all-to-all-start.1 = ((bf16[4,64,4096]{2,1,0:T(8,128)(2,1)}), bf16[4,64,4096]{2,1,0:T(8,128)(2,1)S(1)}, u32[]{:S(2)}, u32[]{:S(2)}) async-start(bf16[4,64,4096]{2,1,0:T(8,128)(2,1)} %broadcast_in_dim.16), calls=%async_computation.1 | async-start | bytes 4194304 | tf_op jit(solution)/shard_map/all_to_all | solution.py:68
  56.7 1.4 %copy-start.3 = (bf16[4,64,4096]{2,1,0:T(8,128)(2,1)}, bf16[4,64,4096]{2,1,0:T(8,128)(2,1)S(1)}, u32[]{:S(2)}) copy-start(bf16[4,64,4096]{2,1,0:T(8,128)(2,1)S(1)} %all-to-all-done.1) | copy-start | bytes 6291460
  58.0 21.2 %copy-start = (s32[1,1,32]{2,1,0:T(1,128)S(1)}, s32[1,1,32]{2,1,0:T(1,128)}, u32[]{:S(2)}) copy-start(s32[1,1,32]{2,1,0:T(1,128)} %param.13) | copy-start | bytes 388
  58.0 21.2 %copy-start.1 = (s32[1,1,32]{2,1,0:T(1,128)S(1)}, s32[1,1,32]{2,1,0:T(1,128)}, u32[]{:S(2)}) copy-start(s32[1,1,32]{2,1,0:T(1,128)} %param.12) | copy-start | bytes 388
  58.0 21.2 %copy-start.2 = (s32[1,1,32]{2,1,0:T(1,128)S(1)}, s32[1,1,32]{2,1,0:T(1,128)}, u32[]{:S(2)}) copy-start(s32[1,1,32]{2,1,0:T(1,128)} %param.14) | copy-start | bytes 388
  102.7 23.0 %copy-start.5 = (bf16[8,4096]{1,0:T(8,128)(2,1)S(1)}, bf16[8,4096]{1,0:T(8,128)(2,1)}, u32[]{:S(2)}) copy-start(bf16[8,4096]{1,0:T(8,128)(2,1)} %param.8) | copy-start | bytes 196612
Sparse Core Ops, SparseCore 0:
  9.8 69.4 all-gather.2

commit v12 on v9

--- a/solution.py
+++ b/solution.py
@@ -78,7 +78,7 @@
 
 def far_exchange(array):
     return lax.all_to_all(array, FAR, 0, 0, tiled=True)
-UNROLL = 16
+UNROLL = 32
 
 
 def pair_kernel(

time: 134 us -> 134 us (level)
  no operation moved by 1% of the time
where the time goes in v12:
time: 134 us; the launch traced here: 133 us
  blocking collectives  70 us (52%)
  waiting for transfers between devices  27.6 us (21%)
  between operations  14.1 us (11%)
  other arithmetic  6.39 us (5%)
  local copies, waits for them, and re-layouts  5.89 us (4%)
  starting transfers between devices  5.05 us (4%)
  Pallas kernels  4.17 us (3%)
    all_to_all x3, blocking collectives, summed_exchange(): lax.all_to_all(parts, PLANES, 0, 0, axis_index_groups=groups, tiled=True)  43.1 us
    all_to_all x1, blocking collectives, far_exchange(): return lax.all_to_all(array, FAR, 0, 0, tiled=True)  26.9 us
    all_gather x1, waiting for transfers between devices, on_device(): blocks = lax.all_gather(blocks, ('z', 'core'), axis=0)  16.4 us
    all_to_all x1, waiting for transfers between devices, near_exchange(): lax.all_to_all(array, PLANES, 0, 0, axis_index_groups=neighbour_blocks(),...  11.2 us
    all_to_all x1, starting transfers between devices, near_exchange(): lax.all_to_all(array, PLANES, 0, 0, axis_index_groups=neighbour_blocks(),...  5.05 us
    pallas_call x1, Pallas kernels, on_device(): pl.pallas_call(pair_kernel, out_shape=jax.ShapeDtypeStruct((members, cell...  4.17 us
  transfers between devices with their start and end apart: 2, of which 2 were waited for; matrix products, arithmetic and copies ran while one was open for 6% of the time, Pallas kernels for 0%

profile of v12, /device:TPU:2, one launch (start us, length us, event | category | flops | bytes accessed | tf_op | source)
XLA Modules:
  0.0 133.3 jit_solution(6439527450240268522)
XLA Ops:
  6.5 0.0 all-gather.3.cloned.1.call-start
  6.5 0.8 fusion.1
  7.3 0.1 copy.21
  7.5 0.1 copy.22
  7.6 1.5 %pad_maximum_fusion = bf16[512,128]{1,0:T(8,128)(2,1)} fusion(bf16[256,128]{1,0:T(8,128)(2,1)} %param.10, bf16[128,128]{1,0:T(8,128)(2,1)S(1)} %copy.22, bf16[128,128]{1,0:T(8,128)(2,1)S(1)} %copy.21), kind=kLoop, calls=%fused_computation.5 | loop fusion | flops 393216 | bytes 262144 | tf_op jit(solution)/shard_map/concatenate | solution.py:156
  9.1 0.0 all-gather.3.cloned.1.call-update
  9.1 0.9 broadcast_in_dim.6
  10.0 26.9 %all_to_all.25 = bf16[8,8,4096]{2,1,0:T(8,128)(2,1)S(1)} all-to-all(bf16[8,8,4096]{2,1,0:T(8,128)(2,1)S(1)} %broadcast_in_dim.6), channel_id=1, replica_groups=mesh['z'=12,'core'=2,'xh'=2,'xl'=2,'yh'=4,'yl'=2] {'xh','yh'}, dimensions={0} | all-to-all | bytes 1048576 | tf_op jit(solution)/shard_map/all_to_all | solution.py:80
  36.9 1.6 %broadcast_in_dim.16 = bf16[4,64,4096]{2,1,0:T(8,128)(2,1)} broadcast(bf16[64,4096]{1,0:T(8,128)(2,1)S(1)} %bitcast.31), dimensions={1,2} | broadcast | bytes 2621440 | tf_op jit(solution)/shard_map/broadcast_in_dim | solution.py:162
  38.5 0.0 copy-start.4
  38.5 5.0 %all-to-all-start.1 = ((bf16[4,64,4096]{2,1,0:T(8,128)(2,1)}), bf16[4,64,4096]{2,1,0:T(8,128)(2,1)S(1)}, u32[]{:S(2)}, u32[]{:S(2)}) async-start(bf16[4,64,4096]{2,1,0:T(8,128)(2,1)} %broadcast_in_dim.16), calls=%async_computation.1 | async-start | bytes 4194304 | tf_op jit(solution)/shard_map/all_to_all | solution.py:74
  43.5 0.0 copy-done.4
  43.5 1.3 %copy.23 = f32[16,128,128]{1,2,0:T(8,128)} copy(f32[16,128,128]{2,1,0:T(8,128)S(1)} %copy-done.4) | data formatting | bytes 2097152 | tf_op args[3]
  45.5 1.3 multiply_bitcast_fusion.taper_ref
  46.9 11.2 %all-to-all-done.1 = bf16[4,64,4096]{2,1,0:T(8,128)(2,1)S(1)} async-done(((bf16[4,64,4096]{2,1,0:T(8,128)(2,1)}), bf16[4,64,4096]{2,1,0:T(8,128)(2,1)S(1)}, u32[]{:S(2)}, u32[]{:S(2)}) %all-to-all-start.1) | async-done | bytes 2097184 | tf_op jit(solution)/shard_map/all_to_all | solution.py:74
  58.0 0.0 copy-start.3
  58.0 0.3 convert_reduce_fusion
  58.4 1.0 copy-done.3
  59.4 0.0 copy-start
  59.4 0.0 copy-start.1
  59.4 0.0 copy-start.2
  59.4 2.1 %fusion.anom_ref = bf16[256,4096]{1,0:T(8,128)(2,1)S(1)} fusion(f32[4096]{0:T(1024)S(1)} %broadcast_multiply_fusion, bf16[4,64,4096]{2,1,0:T(8,128)(2,1)} %copy-done.3), kind=kLoop, calls=%fused_computation.1 | loop fusion | flops 3145728 | bytes 4210688 | tf_op jit(solution)/shard_map/convert_element_type | solution.py:165
  61.5 16.4 %all-gather.3.cloned.1.call-done = bf16[12288,128]{1,0:T(8,128)(2,1)} async-done(((bf16[512,128]{1,0:T(8,128)(2,1)}), bf16[12288,128]{1,0:T(8,128)(2,1)}) %all-gather.3.cloned.1.call-update) | async-done | bytes 3145744 | tf_op jit(solution)/shard_map/all_gather | solution.py:159
  77.9 0.0 copy-done
  78.0 0.0 copy-done.1
  78.0 0.0 copy-done.2
  78.0 4.2 %pairs.1 = bf16[256,4096]{1,0:T(8,128)(2,1)S(1)} custom-call(s32[32]{0:T(128)S(1)} %bitcast.27, s32[32]{0:T(128)S(1)} %bitcast.28, s32[32]{0:T(128)S(1)} %bitcast.29, s32[1]{0:T(128)} %bitcast.25.count_ref, s32[1]{0:T(128)} %bitcast.4.core_ref, bf16[256,4096]{1,0:T(8,128)(2,1)S(1)} %fusion.anom_ref, bf16[24,512,128]{2,1,0:T(8,128)(2,1)} %bitcast.30, ...), custom_call_target="tpu_custom_call" | custom-call | tf_op jit(solution)/shard_map/pairs/pallas_call | solution.py:169
  82.1 18.8 %all_to_all.26 = bf16[4,64,4096]{2,1,0:T(8,128)(2,1)S(1)} all-to-all(bf16[4,64,4096]{2,1,0:T(8,128)(2,1)S(1)} %bitcast.26), channel_id=1, replica_groups={{8,9,16,17},{11,10,19,18},{12,13,20,21},{15,14,23,22},{0,1,24,25},{3,2,..., dimensions={0} | all-to-all | bytes 4194304 | tf_op jit(solution)/shard_map/all_to_all | solution.py:69
  100.9 0.0 copy-start.5
  100.9 0.4 reduce_sum.43
  101.3 14.6 %all_to_all.27 = bf16[4,16,4096]{2,1,0:T(8,128)(2,1)S(1)} all-to-all(bf16[4,16,4096]{2,1,0:T(8,128)(2,1)S(1)} %bitcast.32), channel_id=1, replica_groups={{8,15,0,7},{9,10,1,2},{11,12,3,4},{14,13,6,5},{16,23,24,31},{17,18,25,2..., dimensions={0} | all-to-all | bytes 1048576 | tf_op jit(solution)/shard_map/all_to_all | solution.py:69
  116.0 0.1 reduce_sum.44
  116.0 9.7 %all_to_all.28 = bf16[2,8,4096]{2,1,0:T(8,128)(2,1)S(1)} all-to-all(bf16[2,8,4096]{2,1,0:T(8,128)(2,1)S(1)} %bitcast.33), channel_id=1, replica_groups={{8,11},{12,15},{9,14},{10,13},{16,19},{20,23},{17,22},{18,21},{24,27},{..., dimensions={0} | all-to-all | bytes 262144 | tf_op jit(solution)/shard_map/all_to_all | solution.py:69
  125.8 0.0 copy-done.5
  125.8 0.7 add_convert_fusion
  (4 shorter events, 0.0 us)
Async XLA Ops:
  6.5 71.4 %all-gather.3.cloned.1.call-start = ((), (), s32[]{:S(2)}) async-start(), calls=%async_computation.5 | async-start | bytes 3276800 | tf_op jit(solution)/shard_map/all_gather | solution.py:159
  38.5 5.1 %copy-start.4 = (f32[16,128,128]{2,1,0:T(8,128)S(1)}, f32[16,128,128]{2,1,0:T(8,128)}, u32[]{:S(2)}) copy-start(f32[16,128,128]{2,1,0:T(8,128)} %param.11) | copy-start | bytes 3145732
  38.5 19.5 %all-to-all-start.1 = ((bf16[4,64,4096]{2,1,0:T(8,128)(2,1)}), bf16[4,64,4096]{2,1,0:T(8,128)(2,1)S(1)}, u32[]{:S(2)}, u32[]{:S(2)}) async-start(bf16[4,64,4096]{2,1,0:T(8,128)(2,1)} %broadcast_in_dim.16), calls=%async_computation.1 | async-start | bytes 4194304 | tf_op jit(solution)/shard_map/all_to_all | solution.py:74
  58.0 1.4 %copy-start.3 = (bf16[4,64,4096]{2,1,0:T(8,128)(2,1)}, bf16[4,64,4096]{2,1,0:T(8,128)(2,1)S(1)}, u32[]{:S(2)}) copy-start(bf16[4,64,4096]{2,1,0:T(8,128)(2,1)S(1)} %all-to-all-done.1) | copy-start | bytes 6291460
  59.4 18.6 %copy-start = (s32[1,1,32]{2,1,0:T(1,128)S(1)}, s32[1,1,32]{2,1,0:T(1,128)}, u32[]{:S(2)}) copy-start(s32[1,1,32]{2,1,0:T(1,128)} %param.13) | copy-start | bytes 388
  59.4 18.6 %copy-start.1 = (s32[1,1,32]{2,1,0:T(1,128)S(1)}, s32[1,1,32]{2,1,0:T(1,128)}, u32[]{:S(2)}) copy-start(s32[1,1,32]{2,1,0:T(1,128)} %param.12) | copy-start | bytes 388
  59.4 18.6 %copy-start.2 = (s32[1,1,32]{2,1,0:T(1,128)S(1)}, s32[1,1,32]{2,1,0:T(1,128)}, u32[]{:S(2)}) copy-start(s32[1,1,32]{2,1,0:T(1,128)} %param.14) | copy-start | bytes 388
  100.9 24.8 %copy-start.5 = (bf16[8,4096]{1,0:T(8,128)(2,1)S(1)}, bf16[8,4096]{1,0:T(8,128)(2,1)}, u32[]{:S(2)}) copy-start(bf16[8,4096]{1,0:T(8,128)(2,1)} %param.8) | copy-start | bytes 196612
Sparse Core Ops, SparseCore 0:
  9.8 68.1 all-gather.2
